TPU v7x, 32 devices: a whole 2x2x4 slice. The times are simulated.
32 devices in a mesh: dp: 8 (over z, y), seq: 4 (over x, core).
Axes of the slice: x: 2, y: 2, z: 4, core: 2. Of those that a mesh axis runs over, the one named last changes fastest.
Arguments:
- long_input: bfloat16 [8, 2048, 768], P('dp', 'seq'), may hold values from -6 to 6
- global_input: bfloat16 [8, 230, 768], P('dp'), may hold values from -6 to 6
- lengths: int32 [8], P('dp'), may hold values from 1024 to 2048, as said below
- w_query: bfloat16 [768, 768], replicated, may hold values from -0.21875 to 0.21875
- b_query: float32 [768], replicated, may hold values from -1.25 to 1.25
- w_key: bfloat16 [768, 768], replicated, may hold values from -0.21875 to 0.21875
- w_value: bfloat16 [768, 768], replicated, may hold values from -0.21875 to 0.21875
- b_value: float32 [768], replicated, may hold values from -1.25 to 1.25
- w_out: bfloat16 [768, 768], replicated, may hold values from -6 to 6
- b_out: float32 [768], replicated, may hold values from -1.25 to 1.25
- w_inner: bfloat16 [768, 3072], replicated, may hold values from -0.21875 to 0.21875
- b_inner: float32 [3072], replicated, may hold values from -1.25 to 1.25
- w_outer: bfloat16 [3072, 768], replicated, may hold values from -0.109375 to 0.109375
- b_outer: float32 [768], replicated, may hold values from -1.25 to 1.25
- norm1_gain: float32 [768], replicated, may hold values from 0.5 to 1.5
- norm1_shift: float32 [768], replicated, may hold values from -1.25 to 1.25
- norm2_gain: float32 [768], replicated, may hold values from 0.5 to 1.5
- norm2_shift: float32 [768], replicated, may hold values from -1.25 to 1.25
- rel_table: float32 [169, 12], replicated, may hold values from -6 to 6
- long_cotangent: bfloat16 [8, 2048, 768], P('dp', 'seq'), may hold values from -6 to 6
- global_cotangent: bfloat16 [8, 230, 768], P('dp'), may hold values from -6 to 6
Outputs:
- long_output: bfloat16 [8, 2048, 768], P('dp', 'seq')
- global_output: bfloat16 [8, 230, 768], P('dp')
- long_grad: float32 [8, 2048, 768], P('dp', 'seq')
- global_grad: float32 [8, 230, 768], P('dp')
- grad_w_query: float32 [768, 768], P(('dp', 'seq'))
- grad_b_query: float32 [768], P(('dp', 'seq'))
- grad_w_key: float32 [768, 768], P(('dp', 'seq'))
- grad_w_value: float32 [768, 768], P(('dp', 'seq'))
- grad_b_value: float32 [768], P(('dp', 'seq'))
- grad_w_out: float32 [768, 768], P(('dp', 'seq'))
- grad_b_out: float32 [768], P(('dp', 'seq'))
- grad_w_inner: float32 [768, 3072], P(('dp', 'seq'))
- grad_b_inner: float32 [3072], P(('dp', 'seq'))
- grad_w_outer: float32 [3072, 768], P(('dp', 'seq'))
- grad_b_outer: float32 [768], P(('dp', 'seq'))
- grad_norm1_gain: float32 [768], P(('dp', 'seq'))
- grad_norm1_shift: float32 [768], P(('dp', 'seq'))
- grad_norm2_gain: float32 [768], P(('dp', 'seq'))
- grad_norm2_shift: float32 [768], P(('dp', 'seq'))
- grad_rel_table: float32 [169, 12], replicated
Inputs may be any that keep to these rules, and one draw needn't show every extreme that they name: `lengths`: true long-token count of each document, whose long slots from it up to 2048 are padding; some document has all 2048 slots valid.
All inputs are finite; a program needn't handle non-finite values.
Results may differ from a plain program's by a relative error of at most 0.015.
Values may be sent and summed in bfloat16 or wider, within the bound.
A program may use at most 256 MiB of HBM per device.

v0:
```python
import functools
from typing import NamedTuple

import jax
import jax.numpy as jnp
from jax import lax
from jax.experimental import pallas as pl
from jax.experimental.pallas import tpu as pltpu
from jax.sharding import PartitionSpec as P

HD = 64
R = 84
PAIR = 2 * HD
HALO = 128
REACH = 96
GP = 256
SUB = 256
WINDOW = SUB + 2 * HALO
EPSILON = 1e-05
MASKED = -1e30
F32 = jnp.float32
BF16 = jnp.bfloat16


def dot_t(left, right):
    return lax.dot_general(left, right, (((1,), (1,)), ((), ())), preferred_element_type=F32)


def dot_n(left, right):
    return lax.dot_general(left, right, (((1,), (0,)), ((), ())), preferred_element_type=F32)


def t_dot(left, right):
    return lax.dot_general(left, right, (((0,), (0,)), ((), ())), preferred_element_type=F32)


def band_bias(table_row):
    spread = jnp.broadcast_to(table_row, (SUB, WINDOW))
    return pltpu.roll(spread, 0, 1, stride=1, stride_axis=0)


def diagonal_sums(rows):
    height, width = rows.shape
    while height > 8:
        height //= 2
        rows = rows[:height] + pltpu.roll(rows[height:], width - height, 1)
    row = lax.broadcasted_iota(jnp.int32, rows.shape, 0)
    for bit in (1, 2, 4):
        rows = jnp.where((row & bit) != 0, pltpu.roll(rows, width - bit, 1), rows)
    return jnp.sum(rows, 0, keepdims=True)


def lane_index():
    return lax.broadcasted_iota(jnp.int32, (1, PAIR), 1)


def own_half(head, value):
    low_lanes = lane_index() < HD
    return jnp.where(low_lanes if head == 0 else ~low_lanes, value, jnp.zeros_like(value))


def other_lane(head):
    return HD * (1 - head)


def with_lanes(head, value, columns):
    wide = own_half(head, value.astype(F32))
    lane = lane_index()
    for offset, column in enumerate(columns):
        wide = jnp.where(lane == other_lane(head) + offset, column, wide)
    return wide.astype(BF16)


def in_three(column):
    high = column.astype(BF16).astype(F32)
    middle = (column - high).astype(BF16).astype(F32)
    return (high, middle, column - high - middle)


def key_bias(first, rows, end):
    position = first + lax.broadcasted_iota(jnp.int32, (rows, 1), 0)
    return jnp.where((position >= 0) & (position < end), 0.0, MASKED)


def pick_column(rows, index):
    return jnp.sum(jnp.where(lane_index() == index, rows, 0.0), -1, keepdims=True)


def key_side(head, keys, bias):
    return with_lanes(head, keys, (bias, 1.0, 1.0, 1.0))


def value_side(head, values):
    return with_lanes(head, values, (1.0, 1.0, 1.0))


def softmax_rows(parts, value_parts, head):
    top = functools.reduce(
        jnp.maximum, [jnp.max(part, -1, keepdims=True) for part in parts]
    )
    mixed = sum(
        dot_n(jnp.exp(part - top).astype(BF16), values)
        for part, values in zip(parts, value_parts)
    )
    at = other_lane(head)
    total = mixed[:, at : at + 1]
    return mixed / total, top + jnp.log(total)


def seq_device(steps, seq_count):
    return (lax.axis_index("dp"), lax.rem(lax.axis_index("seq") + steps + seq_count, seq_count))


def row_norm(rows):
    centred = rows - jnp.mean(rows, -1, keepdims=True)
    inverse = lax.rsqrt(jnp.mean(centred * centred, -1, keepdims=True) + EPSILON)
    return centred * inverse, inverse


def put_column(ref, rows, index, column):
    ref[rows] = jnp.where(lane_index() == index, column, ref[rows])


def lanes_of(at):
    return pl.ds(pl.multiple_of(at * PAIR, PAIR), PAIR)


class Sizes(NamedTuple):
    block: int
    count: int
    quarter: int
    seq_count: int
    pairs: int


def attend_kernel(
    sizes,
    len_ref,
    rel_ref,
    long_ref,
    raw_ref,
    wq_ref,
    wk_ref,
    wv_ref,
    bq_ref,
    bv_ref,
    gain_ref,
    shift_ref,
    q_ref,
    kx_ref,
    vx_ref,
    kg_ref,
    vg_ref,
    o_ref,
    l_ref,
    lq_ref,
    glob_ref,
    tab_ref,
    spread,
    wide,
    part_o,
    part_l,
    from_o,
    from_l,
    halo_sends,
    halo_recvs,
    part_sends,
    part_recvs,
):
    block, count, quarter, seq_count, pairs = sizes
    ext = block + 2 * HALO
    seq_index = lax.axis_index("seq")
    scale = jnp.asarray(HD ** (-0.5), BF16)
    low_lanes = lane_index() < HD
    own_keys = slice(HALO, HALO + block)
    own_rows = pl.ds(pl.multiple_of(seq_index * quarter, quarter), quarter)
    neighbours = (seq_index > 0, seq_index < seq_count - 1)
    barrier = pltpu.get_barrier_semaphore()
    for step in range(1, seq_count):
        pl.semaphore_signal(
            barrier,
            inc=1,
            device_id=seq_device(step, seq_count),
            device_id_type=pl.DeviceIdType.MESH,
        )

    def halo_copies(direction):
        source = HALO if direction == 0 else HALO + block - REACH
        dest = HALO + block if direction == 0 else HALO - REACH
        for kind, ref in enumerate((kx_ref, vx_ref)):
            yield pltpu.make_async_remote_copy(
                src_ref=ref.at[source : source + REACH],
                dst_ref=ref.at[dest : dest + REACH],
                send_sem=halo_sends.at[direction, kind],
                recv_sem=halo_recvs.at[direction, kind],
                device_id=seq_device(2 * direction - 1, seq_count),
                device_id_type=pl.DeviceIdType.MESH,
            )

    def part_copies():
        for step in range(1, seq_count):
            device = seq_device(step, seq_count)
            rows = pl.ds(pl.multiple_of(device[1] * quarter, quarter), quarter)
            for kind, (source, dest) in enumerate(((part_o, from_o), (part_l, from_l))):
                yield step, kind, pltpu.make_async_remote_copy(
                    src_ref=source.at[rows],
                    dst_ref=dest.at[step - 1],
                    send_sem=part_sends.at[kind, step - 1],
                    recv_sem=part_recvs.at[kind, step - 1],
                    device_id=device,
                    device_id_type=pl.DeviceIdType.MESH,
                )

    gain, shift = gain_ref[...], shift_ref[...]
    labels, heads = rel_ref.shape
    spread[...] = jnp.full(spread.shape, MASKED, F32)
    spread[:labels, :heads] = rel_ref[...]
    turned = pltpu.roll(spread[...].T, HALO - R, 1)
    for pair in range(pairs):
        tab_ref[pair] = turned[2 * pair : 2 * pair + 2]
    normed_long = (row_norm(long_ref[...].astype(F32))[0] * gain + shift).astype(BF16)
    kx_ref[own_keys] = dot_n(normed_long, wk_ref[...]).astype(BF16)
    vx_ref[own_keys] = (dot_n(normed_long, wv_ref[...]) + bv_ref[...]).astype(BF16)
    pl.semaphore_wait(barrier, seq_count - 1)
    for direction, first in enumerate((HALO - REACH, HALO + block)):

        @pl.when(neighbours[direction])
        def _(direction=direction):
            for copy in halo_copies(direction):
                copy.start()

        outer = slice(0, first) if direction == 0 else slice(first + REACH, ext)
        for ref in (kx_ref, vx_ref):
            ref[outer] = jnp.zeros((HALO - REACH, ref.shape[1]), BF16)

        @pl.when(jnp.logical_not(neighbours[direction]))
        def _(first=first):
            for ref in (kx_ref, vx_ref):
                ref[first : first + REACH] = jnp.zeros((REACH, ref.shape[1]), BF16)

    wide[...] = jnp.zeros_like(wide)
    wide[:count] = raw_ref[...].astype(F32)
    glob_ref[...] = wide[...].astype(BF16)
    normed_glob = (row_norm(wide[...])[0] * gain + shift).astype(BF16)
    kg_ref[...] = dot_n(normed_glob, wk_ref[...]).astype(BF16)
    vg_ref[...] = (dot_n(normed_glob, wv_ref[...]) + bv_ref[...]).astype(BF16)
    q_ref[block:] = (dot_n(normed_glob, wq_ref[...]) + bq_ref[...]).astype(BF16)
    q_ref[:block] = (dot_n(normed_long, wq_ref[...]) + bq_ref[...]).astype(BF16)
    part_l[...] = jnp.zeros_like(part_l)
    l_ref[...] = jnp.zeros_like(l_ref)

    def glob_pair(pair, carry):
        lanes = lanes_of(pair)
        far_bias = key_bias(seq_index * block, block, len_ref[0])
        near_bias = key_bias(seq_index * quarter, quarter, count)
        query = q_ref[block:, lanes] * scale
        outs = []
        for head in range(2):
            q = with_lanes(head, query, (1.0,))
            far = dot_t(q, with_lanes(head, kx_ref[own_keys, lanes], (far_bias,)))
            near = dot_t(q, with_lanes(head, kg_ref[own_rows, lanes], (near_bias,)))
            out, norm = softmax_rows(
                [far, near],
                [
                    with_lanes(head, vx_ref[own_keys, lanes], (1.0,)),
                    with_lanes(head, vg_ref[own_rows, lanes], (1.0,)),
                ],
                head,
            )
            outs.append(out)
            put_column(part_l, slice(None), 2 * pair + head, norm)
        part_o[:, lanes] = jnp.where(low_lanes, outs[0], outs[1]).astype(BF16)
        return carry

    lax.fori_loop(0, pairs, glob_pair, 0)
    for _, _, copy in part_copies():
        copy.start()
    for direction in range(2):

        @pl.when(neighbours[1 - direction])
        def _(direction=direction):
            for copy in halo_copies(direction):
                copy.wait_recv()

    def long_pair(pair, carry):
        lanes = lanes_of(pair)
        long_bias = key_bias(seq_index * block - HALO, ext, len_ref[0])
        glob_bias = key_bias(0, GP, count)
        query = q_ref[:block, lanes] * scale
        outs = []
        for head in range(2):
            q = with_lanes(head, query, (1.0,))
            kx = with_lanes(head, kx_ref[:, lanes], (long_bias,))
            kg = with_lanes(head, kg_ref[:, lanes], (glob_bias,))
            vx, vg = (with_lanes(head, ref[:, lanes], (1.0,)) for ref in (vx_ref, vg_ref))
            bias = band_bias(tab_ref[pair, head : head + 1])
            mixed = []
            for start in range(0, block, SUB):
                rows, keys = slice(start, start + SUB), slice(start, start + WINDOW)
                out, norm = softmax_rows(
                    [dot_t(q[rows], kx[keys]) + bias, dot_t(q[rows], kg)], [vx[keys], vg], head
                )
                mixed.append(out)
                put_column(l_ref, rows, 2 * pair + head, norm)
            outs.append(jnp.concatenate(mixed, 0))
        o_ref[:block, lanes] = jnp.where(low_lanes, outs[0], outs[1]).astype(BF16)
        return carry

    lax.fori_loop(0, pairs, long_pair, 0)
    for _, _, copy in part_copies():
        copy.wait_recv()
    norms = [part_l[own_rows]] + [from_l[step] for step in range(seq_count - 1)]
    outs = [part_o[own_rows]] + [from_o[step] for step in range(seq_count - 1)]
    top = functools.reduce(jnp.maximum, norms)
    shares = [jnp.exp(norm - top) for norm in norms]
    total = sum(shares)
    lq_ref[...] = top + jnp.log(total)
    shares = [share / total for share in shares]
    for at in range(pairs):
        lanes = slice(at * PAIR, (at + 1) * PAIR)
        mixed = 0.0
        for share, out in zip(shares, outs):
            spread = jnp.where(
                low_lanes, share[:, 2 * at : 2 * at + 1], share[:, 2 * at + 1 : 2 * at + 2]
            )
            mixed += spread * out[:, lanes].astype(F32)
        o_ref[block:, lanes] = mixed.astype(BF16)
    for _, _, copy in part_copies():
        copy.wait_send()
    for direction in range(2):

        @pl.when(neighbours[direction])
        def _(direction=direction):
            for copy in halo_copies(direction):
                copy.wait_send()


def attend(sizes, doc_len, rel_table, long_x, glob_x, *weights):
    block, count, quarter, seq_count, pairs = sizes
    width = long_x.shape[1]
    ext = block + 2 * HALO
    whole = pl.BlockSpec(memory_space=pltpu.VMEM)
    shape = jax.ShapeDtypeStruct
    others = seq_count - 1
    return pl.pallas_call(
        functools.partial(attend_kernel, sizes),
        in_specs=[pl.BlockSpec(memory_space=pltpu.SMEM)] + [whole] * 10,
        out_specs=[whole] * 10,
        out_shape=[
            shape((block + GP, width), BF16),
            shape((ext, width), BF16),
            shape((ext, width), BF16),
            shape((GP, width), BF16),
            shape((GP, width), BF16),
            shape((block + quarter, width), BF16),
            shape((block, PAIR), F32),
            shape((quarter, PAIR), F32),
            shape((GP, width), BF16),
            shape((pairs, 2, WINDOW), F32),
        ],
        scratch_shapes=[
            pltpu.VMEM((WINDOW, PAIR), F32),
            pltpu.VMEM((GP, width), F32),
            pltpu.VMEM((GP, width), BF16),
            pltpu.VMEM((GP, PAIR), F32),
            pltpu.VMEM((others, quarter, width), BF16),
            pltpu.VMEM((others, quarter, PAIR), F32),
            pltpu.SemaphoreType.DMA((2, 2)),
            pltpu.SemaphoreType.DMA((2, 2)),
            pltpu.SemaphoreType.DMA((2, others)),
            pltpu.SemaphoreType.DMA((2, others)),
        ],
        compiler_params=pltpu.CompilerParams(
            collective_id=3, has_side_effects=True, vmem_limit_bytes=56 * 2**20
        ),
        name="attend",
    )(doc_len, rel_table, long_x, glob_x, *weights)


class Reducer:
    def __init__(self, rows, split, scratch, pieces=None, order=None):
        self.ids = mesh_ids()
        self.order = order
        self.halves = (slice(0, split), slice(split, rows))
        held, self.from_core, self.from_one, self.from_two, self.from_z = scratch[:5]
        self.local, self.sends, self.recvs = scratch[5:]
        self.pieces, self.held = pieces, held
        self.mine = held.at[self.ids[3]] if pieces is None else held.at[0]

    @staticmethod
    def scratch(rows, width, sides):
        return [
            pltpu.VMEM((sides, 4, 2, 2, rows, width), BF16),
            pltpu.VMEM((4, 2, 2, rows, width), BF16),
            pltpu.VMEM((4, 2, rows, width), BF16),
            pltpu.VMEM((4, rows, width), BF16),
            pltpu.VMEM((3, rows, width), BF16),
            pltpu.SemaphoreType.DMA((4,)),
            pltpu.SemaphoreType.DMA((6, 4)),
            pltpu.SemaphoreType.DMA((6, 4)),
        ]

    def partners(self):
        z, y, x, core = self.ids
        dp, seq = z * 2 + y, x * 2 + core
        near = [(dp, x * 2 + 1 - core), (dp, (1 - x) * 2 + core), (z * 2 + 1 - y, seq)]
        return near + [(lax.rem(z + step, 4) * 2 + y, seq) for step in (1, 2, 3)]

    def target(self, chunk):
        return self.order(chunk) if self.order else lax.rem(self.ids[0] + 1 + chunk, 4)

    def remote(self, source, dest, kind, send_at, recv_at, device):
        return pltpu.make_async_remote_copy(
            src_ref=source,
            dst_ref=dest,
            send_sem=self.sends.at[kind, send_at],
            recv_sem=self.recvs.at[kind, recv_at],
            device_id=device,
            device_id_type=pl.DeviceIdType.MESH,
        )

    def own_copy(self, chunk):
        core, to = self.ids[3], self.target(chunk)
        return pltpu.make_async_copy(
            self.pieces.at[core, to], self.mine.at[to], self.local.at[chunk]
        )

    def core_copy(self, chunk):
        core, to = self.ids[3], self.target(chunk)
        source = (self.held if self.pieces is None else self.pieces).at[1 - core, to]
        return self.remote(source, self.from_core.at[to], 0, chunk, chunk, self.partners()[0])

    def first_copies(self, chunk):
        z, y, x, core = self.ids
        to = self.target(chunk)
        one, two = self.halves
        near = self.partners()
        return (
            self.remote(
                self.mine.at[to, :, 1 - x, one],
                self.from_one.at[to, :, one],
                1,
                chunk,
                chunk,
                near[1],
            ),
            self.remote(
                self.mine.at[to, 1 - y, :, two],
                self.from_one.at[to, :, two],
                2,
                chunk,
                chunk,
                near[2],
            ),
        )

    def second_copies(self, chunk):
        z, y, x, core = self.ids
        to = self.target(chunk)
        one, two = self.halves
        near = self.partners()
        return (
            self.remote(
                self.mine.at[to, 1 - y, x, one],
                self.from_two.at[to, one],
                3,
                chunk,
                chunk,
                near[2],
            ),
            self.remote(
                self.mine.at[to, y, 1 - x, two],
                self.from_two.at[to, two],
                4,
                chunk,
                chunk,
                near[1],
            ),
        )

    def last_copy(self, chunk):
        z, y, x, core = self.ids
        to = self.target(chunk)
        slot = lax.rem(z - to + 4, 4) - 1
        return self.remote(
            self.mine.at[to, y, x],
            self.from_z.at[slot],
            5,
            chunk,
            slot,
            (to * 2 + y, x * 2 + core),
        )

    def arrival(self, slot):
        z, y, x, core = self.ids
        return self.remote(
            self.mine.at[z, y, x], self.from_z.at[slot], 5, slot, slot, self.partners()[3]
        )

    def leaves(self, chunk):
        return self.target(chunk) != self.ids[0]

    def fill(self, to, at, value):
        self.held[at % 2, to, at // 4, at // 2 % 2] = value.astype(BF16)

    def start(self, chunk):
        self.core_copy(chunk).start()
        if self.pieces is not None:
            self.own_copy(chunk).start()

    def add_core(self, chunk):
        to = self.target(chunk)
        if self.pieces is not None:
            self.own_copy(chunk).wait()
        self.core_copy(chunk).wait_recv()

        def add(index, carry):
            at = (to, lax.div(index, 2), lax.rem(index, 2))
            self.mine[at] = self.mine[at] + self.from_core[at]
            return carry

        lax.fori_loop(0, 4, add, 0)
        for copy in self.first_copies(chunk):
            copy.start()

    def add_first(self, chunk):
        z, y, x, core = self.ids
        one, two = self.halves
        to = self.target(chunk)
        for copy in self.first_copies(chunk):
            copy.wait_recv()

        def add(index, carry):
            for at, rows in (((to, index, x), one), ((to, y, index), two)):
                self.mine[at + (rows,)] = self.mine[at + (rows,)] + self.from_one[to, index, rows]
            return carry

        lax.fori_loop(0, 2, add, 0)
        for copy in self.second_copies(chunk):
            copy.start()

    def add_second(self, chunk):
        z, y, x, core = self.ids
        to = self.target(chunk)
        for copy in self.second_copies(chunk):
            copy.wait_recv()

        @pl.when(self.leaves(chunk))
        def _():
            self.mine[to, y, x] = self.mine[to, y, x] + self.from_two[to]
            self.last_copy(chunk).start()

    def finish(self, out):
        z, y, x, core = self.ids
        total = self.mine[z, y, x].astype(F32) + self.from_two[z].astype(F32)
        for slot in range(3):
            self.arrival(slot).wait_recv()
            total += self.from_z[slot].astype(F32)
        out[...] = total
        for chunk in range(4):
            self.core_copy(chunk).wait_send()
            for copy in self.first_copies(chunk) + self.second_copies(chunk):
                copy.wait_send()

            @pl.when(self.leaves(chunk))
            def _(chunk=chunk):
                self.last_copy(chunk).wait_send()


def mesh_ids():
    dp, seq = lax.axis_index("dp"), lax.axis_index("seq")
    return lax.div(dp, 2), lax.rem(dp, 2), lax.div(seq, 2), lax.rem(seq, 2)


def meet(devices):
    barrier = pltpu.get_barrier_semaphore()
    for device in devices:
        pl.semaphore_signal(barrier, inc=1, device_id=device, device_id_type=pl.DeviceIdType.MESH)
    pl.semaphore_wait(barrier, len(devices))


EARLY_PLAN = (
    (2, "add_core", 0),
    (3, "add_core", 1),
    (4, "add_core", 2),
    (5, "add_core", 3),
    (7, "add_first", 0),
    (8, "add_first", 1),
    (9, "add_second", 0),
    (9, "add_first", 2),
    (10, "add_second", 1),
    (10, "add_first", 3),
    (11, "add_second", 2),
    (12, "add_second", 3),
)


def late_kernel(
    sizes,
    planned,
    long_ref,
    glob_ref,
    dq_ref,
    dk_ref,
    dv_ref,
    dmid_ref,
    wq_ref,
    wk_ref,
    wv_ref,
    gain_ref,
    shift_ref,
    table_ref,
    long_out,
    glob_out,
    *rest,
):
    block, count, quarter, seq_count, pairs = sizes
    rows = block + quarter
    width = long_ref.shape[1]
    if planned:
        late_ref, total_ref, *rest = rest
    else:
        gq_ref, gk_ref, gv_ref, total_ref, *rest = rest
    normed_t, every, gather_sends, gather_recvs, *rest = rest
    seq_index = lax.axis_index("seq")
    own_rows = pl.ds(pl.multiple_of(seq_index * quarter, quarter), quarter)
    others = [seq_device(step, seq_count) for step in range(1, seq_count)]

    def gathers():
        for step, device in enumerate(others):
            yield pltpu.make_async_remote_copy(
                src_ref=every.at[own_rows],
                dst_ref=every.at[own_rows],
                send_sem=gather_sends.at[step],
                recv_sem=gather_recvs.at[step],
                device_id=device,
                device_id_type=pl.DeviceIdType.MESH,
            )

    if planned:
        kept, arrived, table_sends, table_recvs, *rest = rest
        reducer = Reducer(rest[0].shape[-2], 32, rest)
        z, y, x, core = mesh_ids()
        partners = reducer.partners()[:3] + [
            ((z + 1 - 2 * lax.rem(z, 2)) * 2 + y, lax.axis_index("seq")),
            (lax.rem(z + 2, 4) * 2 + y, lax.axis_index("seq")),
        ]

        def table_copy(stage):
            return pltpu.make_async_remote_copy(
                src_ref=kept.at[stage],
                dst_ref=arrived.at[stage],
                send_sem=table_sends.at[stage],
                recv_sem=table_recvs.at[stage],
                device_id=partners[stage],
                device_id_type=pl.DeviceIdType.MESH,
            )

        def table_step(stage):
            table_copy(stage).wait_recv()
            kept[stage + 1] = kept[stage] + arrived[stage]
            if stage < 4:
                table_copy(stage + 1).start()

    meet(others + (reducer.partners()[2:] if planned else []))
    everything = jnp.concatenate([long_ref[...], glob_ref[own_rows]], 0).astype(F32)
    hat, inverse = row_norm(everything)
    normed_t[...] = (hat * gain_ref[...] + shift_ref[...]).astype(BF16).T
    if planned:
        piece = width // 32
        blank = jnp.zeros((8, width), F32)
        def weight_rows(chunk):
            to = reducer.target(chunk)
            some = normed_t[pl.ds(pl.multiple_of(to * 8 * piece, 64), 8 * piece)]
            parts = [dot_n(some, ref[...]) for ref in (dq_ref, dk_ref, dv_ref)]
            for at in range(8):
                rows_at = slice(at * piece, (at + 1) * piece)
                reducer.fill(
                    to, at, jnp.concatenate([part[rows_at] for part in parts] + [blank], 0)
                )
            reducer.start(chunk)

        weight_rows(0)
        weight_rows(1)
        reducer.add_core(0)
        weight_rows(2)
        reducer.add_core(1)
        weight_rows(3)
        grads = dot_t(dq_ref[...], wq_ref[...])
        reducer.add_first(0)
        reducer.add_core(2)
        grads += dot_t(dk_ref[...], wk_ref[...]) + dot_t(dv_ref[...], wv_ref[...])
        reducer.add_first(1)
        reducer.add_core(3)
        reducer.add_second(0)
    else:
        for ref, out in ((dq_ref, gq_ref), (dk_ref, gk_ref), (dv_ref, gv_ref)):
            out[...] = dot_n(normed_t[...], ref[...]).astype(BF16)
        grads = (
            dot_t(dq_ref[...], wq_ref[...])
            + dot_t(dk_ref[...], wk_ref[...])
            + dot_t(dv_ref[...], wv_ref[...])
        )
    scaled = grads * gain_ref[...]
    total = dmid_ref[...] + inverse * (
        scaled
        - jnp.mean(scaled, -1, keepdims=True)
        - hat * jnp.mean(scaled * hat, -1, keepdims=True)
    )
    every[own_rows] = total[block:].astype(BF16)
    for copy in gathers():
        copy.start()
    long_out[...] = total[:block]
    sums = [
        column_sum(part)
        for part in (dq_ref[...].astype(F32), dv_ref[...].astype(F32), grads * hat, grads)
    ]
    heads = 2 * pairs
    first = kept.at[0] if planned else total_ref
    first[...] = jnp.zeros(first.shape, F32)
    for pair in range(pairs):
        first[2 * pair : 2 * pair + 2, :WINDOW] = table_ref[pair]
    for at, vector in enumerate(sums):
        first[heads + at : heads + at + 1] = vector
    if planned:
        table_copy(0).start()
        for number, (act, chunk) in enumerate(LATE_TAIL):
            getattr(reducer, act)(chunk)
            table_step(number)
        total_ref[...] = kept[5]
        reducer.finish(late_ref)
        for stage in range(5):
            table_copy(stage).wait_send()
    for copy in gathers():
        copy.wait_recv()
    glob_out[...] = every[:count].astype(F32)
    for copy in gathers():
        copy.wait_send()


LATE_TAIL = (
    ("add_first", 2),
    ("add_second", 1),
    ("add_first", 3),
    ("add_second", 2),
    ("add_second", 3),
)


def last_part(sizes, planned, long_x, glob_x, dq, dk, dv, dmid, wq, wk, wv, gain, shift, table):
    block, count, quarter, seq_count, pairs = sizes
    rows, width = dq.shape
    others = seq_count - 1
    whole = pl.BlockSpec(memory_space=pltpu.VMEM)
    shape = jax.ShapeDtypeStruct
    sums = shape(((2 * pairs + 4 + 7) // 8 * 8, width), F32)
    outs = [shape((block, width), F32), shape((count, width), F32)]
    scratch = [
        pltpu.VMEM((width, rows), BF16),
        pltpu.VMEM((GP, width), BF16),
        pltpu.SemaphoreType.DMA((others,)),
        pltpu.SemaphoreType.DMA((others,)),
    ]
    if planned:
        piece = width // 32
        part = 3 * piece + 8
        outs += [shape((part, width), F32), sums]
        scratch += [
            pltpu.VMEM((6,) + sums.shape, F32),
            pltpu.VMEM((5,) + sums.shape, F32),
            pltpu.SemaphoreType.DMA((5,)),
            pltpu.SemaphoreType.DMA((5,)),
        ] + Reducer.scratch(part, width, 2)
    else:
        outs += [shape((width, width), BF16)] * 3 + [sums]
    return pl.pallas_call(
        functools.partial(late_kernel, sizes, planned),
        in_specs=[whole] * 12,
        out_specs=[whole] * len(outs),
        out_shape=outs,
        scratch_shapes=scratch,
        compiler_params=pltpu.CompilerParams(
            collective_id=2, has_side_effects=True, vmem_limit_bytes=60 * 2**20
        ),
        name="last_part",
    )(long_x, glob_x, dq, dk, dv, dmid, wq, wk, wv, gain, shift, table)


def small_kernel(heads, early_ref, late_ref, outer_ref, inner_ref, sums_ref, *outs):
    g_query, g_key, g_value, g_out, g_inner, g_outer, *vectors, table = outs
    device = lax.axis_index("dp") * lax.axis_size("seq") + lax.axis_index("seq")
    piece, width = g_query.shape
    for at, out in enumerate((g_query, g_key, g_value)):
        out[...] = late_ref[at * piece : (at + 1) * piece]
    g_out[...] = early_ref[2 * piece : 3 * piece]
    g_outer[...] = outer_ref[...]
    for source, first, chunk in (
        (inner_ref, 0, 0),
        (inner_ref, piece, 3),
        (early_ref, 0, 1),
        (early_ref, piece, 2),
    ):
        g_inner[:, chunk * width : (chunk + 1) * width] = source[first : first + piece]

    def entries(row, at, length):
        return pltpu.roll(row, width - at * length, 1)[0, :length]

    b_query, b_value, b_out, b_outer, gain_one, shift_one, gain_two, shift_two, b_inner = vectors
    for at, out in enumerate((b_query, b_value, gain_one, shift_one)):
        out[...] = entries(sums_ref[heads + at : heads + at + 1], device, piece)
    for at, out in enumerate((b_out, b_outer, gain_two, shift_two)):
        row = 3 * piece + at
        out[...] = entries(early_ref[row : row + 1], device, piece)
    row = pl.ds(3 * piece + 4 + lax.div(device, 8), 1)
    b_inner[...] = entries(early_ref[row], lax.rem(device, 8), 4 * piece)
    labels = table.shape[0]
    turned = pltpu.roll(sums_ref[:, :WINDOW], WINDOW - HALO + R, 1).T
    table[...] = turned[:labels, :heads]


def small_results(heads, early, late, outer, inner, sums):
    width = early.shape[1]
    piece = width // 32
    shape = jax.ShapeDtypeStruct
    whole = pl.BlockSpec(memory_space=pltpu.VMEM)
    outs = [shape((piece, width), F32)] * 4
    outs += [shape((piece, 4 * width), F32), shape((4 * piece, width), F32)]
    outs += [shape((piece,), F32)] * 8 + [shape((4 * piece,), F32)]
    outs += [shape((2 * R + 1, heads), F32)]
    return pl.pallas_call(
        functools.partial(small_kernel, heads),
        in_specs=[whole] * 5,
        out_specs=[whole] * len(outs),
        out_shape=outs,
        name="small_results",
    )(early, late, outer, inner, sums)


def has_plan():
    return (lax.axis_size("dp"), lax.axis_size("seq")) == (8, 4)


GELU_A = 0.7978845608028654
GELU_B = 0.044715


def gate_both(u):
    square = u * u
    turned = jnp.tanh(GELU_A * u * (1.0 + GELU_B * square))
    half = 0.5 * (1.0 + turned)
    slope = half + 0.5 * u * (1.0 - turned * turned) * (
        GELU_A * (1.0 + 3.0 * GELU_B * square)
    )
    return u * half, slope


def column_sum(rows):
    return jnp.sum(rows, 0, keepdims=True)


def ffn_kernel(
    sizes,
    planned,
    len_ref,
    attn_ref,
    long_ref,
    glob_ref,
    dlong_ref,
    dglob_ref,
    lq_ref,
    wo_ref,
    bo_ref,
    gain_ref,
    shift_ref,
    wi_ref,
    bi_ref,
    wr_ref,
    br_ref,
    long_out,
    glob_out,
    dmid_ref,
    do_ref,
    dog_ref,
    ldg_ref,
    *rest,
):
    block, count, quarter, seq_count, pairs = sizes
    if planned:
        pieces_ref, outer_ref, inner_ref, *rest = rest
    else:
        g_outer_ref, g_inner_ref, g_out_ref, vec_ref, *rest = rest
    (
        mid,
        y_sum,
        df_sum,
        normed,
        normed_t,
        dy,
        vectors,
        biases,
        every_do,
        every_ld,
        every_out,
        gather_sends,
        gather_recvs,
        *rest,
    ) = rest
    if planned:
        even, *rest = rest
        outer = Reducer(rest[0].shape[-2], 48, rest[:8], order=chunk_of)
        inner = Reducer(rest[8].shape[-2], 16, rest[8:])
    step = pl.program_id(0)
    chunk = chunk_of(step)
    seq_index = lax.axis_index("seq")
    own_rows = pl.ds(pl.multiple_of(seq_index * quarter, quarter), quarter)
    width = mid.shape[1]
    piece = width // 32

    def gathers(kinds):
        for seq_step in range(1, seq_count):
            for kind in kinds:
                every = (every_do, every_ld, every_out)[kind]
                yield pltpu.make_async_remote_copy(
                    src_ref=every.at[own_rows],
                    dst_ref=every.at[own_rows],
                    send_sem=gather_sends.at[kind, seq_step - 1],
                    recv_sem=gather_recvs.at[kind, seq_step - 1],
                    device_id=seq_device(seq_step, seq_count),
                    device_id_type=pl.DeviceIdType.MESH,
                )

    def act(now):
        if planned:
            for at, reducer, name, part in FFN_PLAN:
                if at == now:
                    getattr((outer, inner)[reducer], name)(part)

    def act_in_step(point):
        if planned:
            for now in range(4):
                if any(at == (now, point) for at, _, _, _ in FFN_PLAN):

                    @pl.when(step == now)
                    def _(now=now):
                        act((now, point))

    @pl.when(step == 0)
    def _():
        others = [seq_device(seq_step, seq_count) for seq_step in range(1, seq_count)]
        meet(others + (outer.partners()[2:] if planned else []))
        projected = dot_n(attn_ref[...], wo_ref[...]) + bo_ref[...]
        mid[:block] = long_ref[...].astype(F32) + projected[:block]
        mid[block:] = glob_ref[own_rows].astype(F32) + projected[block:]
        hat, _ = row_norm(mid[...])
        normed[...] = (hat * gain_ref[...] + shift_ref[...]).astype(BF16)
        normed_t[...] = normed[...].T
        position = seq_index * block + lax.broadcasted_iota(jnp.int32, (block, 1), 0)
        dy[:block] = jnp.where(
            position < len_ref[0], dlong_ref[...].astype(F32), 0.0
        ).astype(BF16)
        y_sum[:GP] = jnp.zeros((GP, width), F32)
        y_sum[:count] = dglob_ref[...].astype(F32)
        dy[block:] = y_sum[own_rows].astype(BF16)
        vectors[1:2] = column_sum(dy[...].astype(F32))
        y_sum[...] = mid[...] + br_ref[...]
        df_sum[...] = jnp.zeros_like(df_sum)
        for at in range(4):
            biases[at] = bi_ref[at * width : (at + 1) * width].reshape(1, width)

    act_in_step(0)
    active, slope = gate_both(dot_n(normed[...], wi_ref[...]) + biases[chunk])
    active = active.astype(BF16)
    g_outer = t_dot(active, dy[...])
    if planned:
        for at in range(8):
            outer.fill(chunk, at, g_outer[at * 4 * piece : (at + 1) * 4 * piece])
        outer.start(step)
    else:
        g_outer_ref[...] = g_outer.astype(BF16)
    y_sum[...] += dot_n(active, wr_ref[...])
    hidden = dot_t(dy[...], wr_ref[...]) * slope
    for at in range(4):

        @pl.when(chunk == at)
        def _(at=at):
            vectors[4 + at : 5 + at] = column_sum(hidden)

    hidden = hidden.astype(BF16)
    act_in_step(1)
    df_sum[...] += dot_t(hidden, wi_ref[...])
    g_inner = dot_n(normed_t[...], hidden)
    if planned:

        @pl.when(lax.rem(step, 2) == 0)
        def _():
            even[...] = g_inner

        def halves(at):
            part = slice(at * piece, (at + 1) * piece)
            return jnp.concatenate([even[part], g_inner[part]], 0)

        @pl.when(step == 1)
        def _():
            for at in range(32):
                inner.fill(at // 8, at % 8, halves(at))
            for part in range(4):
                inner.start(part)

        @pl.when(step == 3)
        def _():
            for at in range(32):
                pieces_ref[at % 2, at // 8, at // 4 % 2, at // 2 % 2, : 2 * piece] = halves(
                    at
                ).astype(BF16)

    else:
        g_inner_ref[...] = g_inner.astype(BF16)

    def norm_back(rows):
        hat, inverse = row_norm(mid[rows])
        df = df_sum[rows]
        scaled = df * gain_ref[...]
        dmid = dy[rows].astype(F32) + inverse * (
            scaled
            - jnp.mean(scaled, -1, keepdims=True)
            - hat * jnp.mean(scaled * hat, -1, keepdims=True)
        )
        dmid_ref[rows] = dmid
        low = dmid.astype(BF16)
        grad_o = dot_t(low, wo_ref[...]).astype(BF16)
        do_ref[rows] = grad_o
        return [column_sum(dmid), column_sum(df * hat), column_sum(df)], low, grad_o

    @pl.when(step == 3)
    def _():
        glob_sums, glob_low, grad_o = norm_back(slice(block, block + quarter))
        every_do[own_rows] = grad_o
        both = grad_o.astype(F32) * attn_ref[block:].astype(F32)
        stats = lq_ref[...]
        for head in range(2 * pairs):
            lanes = slice(head // 2 * PAIR, head // 2 * PAIR + PAIR)
            delta = jnp.sum(own_half(head % 2, both[:, lanes]), -1, keepdims=True)
            stats = jnp.where(lane_index() == HD + head, delta, stats)
        every_ld[own_rows] = stats
        every_out[own_rows] = y_sum[block:].astype(BF16)
        for copy in gathers((0, 1, 2)):
            copy.start()
        act((4, 0))
        position = seq_index * block + lax.broadcasted_iota(jnp.int32, (block, 1), 0)
        long_out[...] = jnp.where(position < len_ref[0], y_sum[:block], 0.0).astype(BF16)
        long_sums, long_low, _ = norm_back(slice(0, block))
        for at, one, two in zip((0, 2, 3), long_sums, glob_sums):
            vectors[at : at + 1] = one + two
        act((4, 1))
        g_out = t_dot(attn_ref[...], jnp.concatenate([long_low, glob_low], 0))
        if planned:
            for at in range(32):
                pieces_ref[at % 2, at // 8, at // 4 % 2, at // 2 % 2, 2 * piece :] = (
                    jnp.concatenate(
                        [g_out[at * piece : (at + 1) * piece], vectors[...]], 0
                    ).astype(BF16)
                )
            act((4, 2))
            outer.finish(outer_ref)
            inner.finish(inner_ref)
        else:
            g_out_ref[...] = g_out.astype(BF16)
            vec_ref[...] = vectors[...]
        for copy in gathers((0, 1, 2)):
            copy.wait_recv()
        dog_ref[...] = every_do[...]
        ldg_ref[...] = every_ld[...]
        glob_out[...] = every_out[:count]
        for copy in gathers((0, 1, 2)):
            copy.wait_send()


OUTER, INNER = 0, 1
FFN_PLAN = (
    ((1, 0), OUTER, "add_core", 0),
    ((2, 0), OUTER, "add_first", 0),
    ((2, 0), OUTER, "add_core", 1),
    ((2, 1), OUTER, "add_second", 0),
    ((2, 1), INNER, "add_core", 0),
    ((2, 1), INNER, "add_core", 1),
    ((2, 1), INNER, "add_core", 2),
    ((2, 1), INNER, "add_core", 3),
    ((3, 0), OUTER, "add_first", 1),
    ((3, 0), OUTER, "add_core", 2),
    ((3, 1), OUTER, "add_second", 1),
    ((3, 1), INNER, "add_first", 0),
    ((3, 1), INNER, "add_first", 1),
    ((4, 0), OUTER, "add_core", 3),
    ((4, 0), OUTER, "add_first", 2),
    ((4, 0), INNER, "add_second", 0),
    ((4, 0), INNER, "add_first", 2),
    ((4, 0), INNER, "add_second", 1),
    ((4, 0), INNER, "add_first", 3),
    ((4, 1), OUTER, "add_second", 2),
    ((4, 1), OUTER, "add_first", 3),
    ((4, 1), INNER, "add_second", 2),
    ((4, 2), OUTER, "add_second", 3),
    ((4, 2), INNER, "add_second", 3),
)


def chunk_of(step):
    return jnp.where(step == 0, 0, jnp.where(step == 1, 3, step - 1))


def feed_forward(sizes, planned, doc_len, attn, long_x, glob_x, dlong, dglob, lq, *weights):
    block, count, quarter, seq_count, pairs = sizes
    wo, bo, gain, shift, wi, bi, wr, br = weights
    width, hidden = wi.shape
    chunk = hidden // 4
    rows = block + quarter
    whole = pl.BlockSpec(memory_space=pltpu.VMEM)
    shape = jax.ShapeDtypeStruct
    in_specs = [pl.BlockSpec(memory_space=pltpu.SMEM)] + [whole] * 10
    in_specs += [
        pl.BlockSpec((width, chunk), lambda c: (0, chunk_of(c))),
        whole,
        pl.BlockSpec((chunk, width), lambda c: (chunk_of(c), 0)),
        whole,
    ]
    outs = [
        shape((block, width), BF16),
        shape((count, width), BF16),
        shape((rows, width), F32),
        shape((rows, width), BF16),
        shape((GP, width), BF16),
        shape((GP, PAIR), F32),
    ]
    out_specs = [whole] * 6
    others = seq_count - 1
    scratch = [
        pltpu.VMEM((rows, width), F32),
        pltpu.VMEM((rows, width), F32),
        pltpu.VMEM((rows, width), F32),
        pltpu.VMEM((rows, width), BF16),
        pltpu.VMEM((width, rows), BF16),
        pltpu.VMEM((rows, width), BF16),
        pltpu.VMEM((8, width), F32),
        pltpu.VMEM((4, 1, chunk), F32),
        pltpu.VMEM((GP, width), BF16),
        pltpu.VMEM((GP, PAIR), F32),
        pltpu.VMEM((GP, width), BF16),
        pltpu.SemaphoreType.DMA((3, others)),
        pltpu.SemaphoreType.DMA((3, others)),
    ]
    if planned:
        part, piece = hidden // 32, width // 32
        outs += [
            shape((2, 4, 2, 2, 3 * piece + 8, width), BF16),
            shape((part, width), F32),
            shape((2 * piece, width), F32),
        ]
        out_specs += [whole] * 3
        scratch += [
            pltpu.VMEM((width, chunk), F32),
        ]
        scratch += Reducer.scratch(part, width, 2) + Reducer.scratch(2 * piece, width, 2)
    else:
        outs += [
            shape((hidden, width), BF16),
            shape((width, hidden), BF16),
            shape((width, width), BF16),
            shape((8, width), F32),
        ]
        out_specs += [
            pl.BlockSpec((chunk, width), lambda c: (chunk_of(c), 0)),
            pl.BlockSpec((width, chunk), lambda c: (0, chunk_of(c))),
            whole,
            whole,
        ]
    return pl.pallas_call(
        functools.partial(ffn_kernel, sizes, planned),
        grid=(4,),
        in_specs=in_specs,
        out_specs=out_specs,
        out_shape=outs,
        scratch_shapes=scratch,
        compiler_params=pltpu.CompilerParams(
            collective_id=4, has_side_effects=True, vmem_limit_bytes=62 * 2**20
        ),
        name="feed_forward",
    )(doc_len, attn, long_x, glob_x, dlong, dglob, lq, wo, bo, gain, shift, wi, bi, wr, br)


def back_kernel(
    sizes,
    early_rows,
    len_ref,
    tab_ref,
    q_ref,
    kx_ref,
    vx_ref,
    kg_ref,
    vg_ref,
    o_ref,
    do_ref,
    l_ref,
    dog_ref,
    ldg_ref,
    *rest,
):
    block, count, quarter, seq_count, pairs = sizes
    reduces = early_rows > 0
    if reduces:
        pieces_ref, rest = rest[0], rest[1:]
    dq_ref, dk_ref, dv_ref, dtab_ref, *rest = rest
    if reduces:
        early_ref, rest = rest[0], rest[1:]
    (
        dkx,
        dvx,
        dkg,
        dvg,
        q_send,
        q_recv,
        kv_send,
        kv_recv,
        halo_send,
        halo_recv,
        glob_sends,
        glob_recvs,
        halo_sends,
        halo_recvs,
        *rest,
    ) = rest
    number = pl.program_id(0)
    pair = lax.rem(number, pairs)
    seq_index = lax.axis_index("seq")
    reducer = Reducer(early_rows, 16, rest, pieces=pieces_ref) if reduces else None
    scale = HD ** (-0.5)
    low_lanes = lane_index() < HD
    own_keys = slice(HALO, HALO + block)
    own_rows = pl.ds(pl.multiple_of(seq_index * quarter, quarter), quarter)

    def glob_copies(kind, at):
        source, dest = ((q_send, q_recv), (kv_send, kv_recv))[kind]
        for step in range(1, seq_count):
            device = seq_device(step, seq_count)
            yield pltpu.make_async_remote_copy(
                src_ref=source.at[device[1], at],
                dst_ref=dest.at[step - 1, at],
                send_sem=glob_sends.at[kind, step - 1, at],
                recv_sem=glob_recvs.at[kind, step - 1, at],
                device_id=device,
                device_id_type=pl.DeviceIdType.MESH,
            )

    def halo_copy(direction, at):
        return pltpu.make_async_remote_copy(
            src_ref=halo_send.at[direction, at],
            dst_ref=halo_recv.at[direction, at],
            send_sem=halo_sends.at[direction, at],
            recv_sem=halo_recvs.at[direction, at],
            device_id=seq_device(2 * direction - 1, seq_count),
            device_id_type=pl.DeviceIdType.MESH,
        )

    has_low, has_high = seq_index > 0, seq_index < seq_count - 1
    sends_to = (has_low, has_high)
    gets_from = (has_high, has_low)

    def close_pair(at):
        lanes = lanes_of(at)
        for direction in range(2):

            @pl.when(gets_from[direction])
            def _(direction=direction):
                halo_copy(direction, at).wait_recv()

        for kind, (total, out) in enumerate(((dkx, dk_ref), (dvx, dv_ref))):
            first, last = HALO + REACH, HALO + block - REACH
            out[:REACH, lanes] = (
                total[at, HALO:first] + halo_recv[1, at, kind].astype(F32)
            ).astype(BF16)
            out[REACH : block - REACH, lanes] = total[at, first:last].astype(BF16)
            out[block - REACH : block, lanes] = (
                total[at, last : HALO + block] + halo_recv[0, at, kind].astype(F32)
            ).astype(BF16)
        sums = []
        for kind, (source, dest) in enumerate(((q_send, q_recv), (kv_send, kv_recv))):
            total = source[seq_index, at].astype(F32)
            for step, copy in enumerate(glob_copies(kind, at)):
                copy.wait_recv()
                total += dest[step, at].astype(F32)
            sums.append(total.astype(BF16))
        dq_ref[block:, lanes] = sums[0]
        dk_ref[block:, lanes] = sums[1][:, :PAIR]
        dv_ref[block:, lanes] = sums[1][:, PAIR:]

    def run_plan(now):
        for at, act, chunk in EARLY_PLAN:
            if now == at:
                getattr(reducer, act)(chunk)

    @pl.when(number == 0)
    def _():
        others = [seq_device(step, seq_count) for step in range(1, seq_count)]
        meet(others + (reducer.partners()[2:] if reduces else []))
        if reduces:
            for chunk in range(4):
                reducer.start(chunk)
        for direction in range(2):

            @pl.when(jnp.logical_not(gets_from[direction]))
            def _(direction=direction):
                halo_recv[direction] = jnp.zeros_like(halo_recv[direction])

    if reduces:
        for now in range(1, 2 * pairs):
            if any(at == now for at, _, _ in EARLY_PLAN):

                @pl.when(number == now)
                def _(now=now):
                    run_plan(now)

    @pl.when(number < pairs)
    def _():
        long_bias = key_bias(seq_index * block, block, len_ref[0])
        near_bias = key_bias(seq_index * quarter, quarter, count)
        query = q_ref[block:] * jnp.asarray(scale, BF16)
        grad_o = dog_ref[...]
        far_k, far_v = kx_ref[own_keys], vx_ref[own_keys]
        near_k, near_v = kg_ref[own_rows], vg_ref[own_rows]
        outs, kept = [], []
        for head in range(2):
            norm = in_three(-pick_column(ldg_ref[...], 2 * pair + head))
            delta = in_three(-pick_column(ldg_ref[...], HD + 2 * pair + head))
            qa = with_lanes(head, query, (1.0,) + norm)
            doa = with_lanes(head, grad_o, delta)
            far = jnp.exp(dot_t(qa, key_side(head, far_k, long_bias)))
            near = jnp.exp(dot_t(qa, key_side(head, near_k, near_bias)))
            far_ds = (far * dot_t(doa, value_side(head, far_v))).astype(BF16)
            near_ds = (near * dot_t(doa, value_side(head, near_v))).astype(BF16)
            outs.append(dot_n(far_ds, far_k) + dot_n(near_ds, near_k))
            kept.append(
                (
                    own_half(head, query),
                    own_half(head, grad_o),
                    far.astype(BF16),
                    near.astype(BF16),
                    far_ds,
                    near_ds,
                )
            )
        own_q, own_do, far, near, far_ds, near_ds = (
            jnp.concatenate(part, 0) for part in zip(*kept)
        )
        for total, edge in ((dkx, own_keys), (dvx, own_keys)):
            total[pair, :HALO] = jnp.zeros((HALO, PAIR), F32)
            total[pair, HALO + block :] = jnp.zeros((HALO, PAIR), F32)
        dkx[pair, own_keys] = t_dot(far_ds, own_q)
        dvx[pair, own_keys] = t_dot(far, own_do)
        dkg[pair] = jnp.zeros((GP, PAIR), F32)
        dvg[pair] = jnp.zeros((GP, PAIR), F32)
        dkg[pair, own_rows] = t_dot(near_ds, own_q)
        dvg[pair, own_rows] = t_dot(near, own_do)
        glob_dq = (jnp.where(low_lanes, outs[0], outs[1]) * scale).astype(BF16)
        q_send[:, pair] = glob_dq.reshape(seq_count, quarter, PAIR)
        for copy in glob_copies(0, pair):
            copy.start()

    @pl.when(number >= pairs)
    def _():
        long_bias = key_bias(seq_index * block - HALO, block + 2 * HALO, len_ref[0])
        glob_bias = key_bias(0, GP, count)
        query = q_ref[:block] * jnp.asarray(scale, BF16)
        grad_o = do_ref[...]
        both = grad_o.astype(F32) * o_ref[...].astype(F32)
        heads = []
        for head in range(2):
            norm = in_three(-pick_column(l_ref[...], 2 * pair + head))
            delta = in_three(-jnp.sum(own_half(head, both), -1, keepdims=True))
            heads.append(
                dict(
                    q=own_half(head, query),
                    do=own_half(head, grad_o),
                    qa=with_lanes(head, query, (1.0,) + norm),
                    doa=with_lanes(head, grad_o, delta),
                    kxa=key_side(head, kx_ref[...], long_bias),
                    vxa=value_side(head, vx_ref[...]),
                    kga=key_side(head, kg_ref[...], glob_bias),
                    vga=value_side(head, vg_ref[...]),
                    bias=band_bias(tab_ref[0, head : head + 1]),
                )
            )
        table_sums = [0.0, 0.0]
        grads_q = []
        for start in range(0, block, SUB):
            rows, keys = slice(start, start + SUB), slice(start, start + WINDOW)
            outs, probs, grads = [], [], []
            for head, own in enumerate(heads):
                band = jnp.exp(dot_t(own["qa"][rows], own["kxa"][keys]) + own["bias"])
                band_ds = band * dot_t(own["doa"][rows], own["vxa"][keys])
                table_sums[head] += band_ds
                glob = jnp.exp(dot_t(own["qa"][rows], own["kga"]))
                glob_ds = (glob * dot_t(own["doa"][rows], own["vga"])).astype(BF16)
                band_ds = band_ds.astype(BF16)
                outs.append(dot_n(band_ds, kx_ref[keys]) + dot_n(glob_ds, kg_ref[...]))
                probs.append((band.astype(BF16), glob.astype(BF16)))
                grads.append((band_ds, glob_ds))
            grads_q.append(jnp.where(low_lanes, outs[0], outs[1]))
            own_q = jnp.concatenate([own["q"][rows] for own in heads], 0)
            own_do = jnp.concatenate([own["do"][rows] for own in heads], 0)
            band, glob = (jnp.concatenate(part, 0) for part in zip(*probs))
            band_ds, glob_ds = (jnp.concatenate(part, 0) for part in zip(*grads))
            dkx[pair, keys] += t_dot(band_ds, own_q)
            dvx[pair, keys] += t_dot(band, own_do)
            dkg[pair] += t_dot(glob_ds, own_q)
            dvg[pair] += t_dot(glob, own_do)
        for kind, total in enumerate((dkg, dvg)):
            kv_send[:, pair, :, kind * PAIR : (kind + 1) * PAIR] = (
                total[pair].astype(BF16).reshape(seq_count, quarter, PAIR)
            )
        for copy in glob_copies(1, pair):
            copy.start()
        for kind, total in enumerate((dkx, dvx)):
            for direction, first in enumerate((HALO - REACH, HALO + block)):
                halo_send[direction, pair, kind] = total[pair, first : first + REACH].astype(BF16)
        for direction in range(2):

            @pl.when(sends_to[direction])
            def _(direction=direction):
                halo_copy(direction, pair).start()

        dq_ref[:block, lanes_of(pair)] = (jnp.concatenate(grads_q, 0) * scale).astype(BF16)
        for head in range(2):
            dtab_ref[pair, head : head + 1] = diagonal_sums(table_sums[head])

    @pl.when(number > pairs)
    def _():
        close_pair(pair - 1)

    @pl.when(number == 2 * pairs - 1)
    def _():
        if reduces:
            run_plan(2 * pairs)
        close_pair(pairs - 1)
        for at in range(pairs):
            for kind in range(2):
                for copy in glob_copies(kind, at):
                    copy.wait_send()
            for direction in range(2):

                @pl.when(sends_to[direction])
                def _(direction=direction, at=at):
                    halo_copy(direction, at).wait_send()

        if reduces:
            reducer.finish(early_ref)


def attend_back(sizes, doc_len, table, q, kx, vx, kg, vg, o, do, l, dog, ldg, pieces=None):
    block, count, quarter, seq_count, pairs = sizes
    width = q.shape[1]
    early_rows = 0 if pieces is None else pieces.shape[-2]
    ext = block + 2 * HALO
    cols = lambda rows: pl.BlockSpec((rows, PAIR), lambda i: (0, lax.rem(i, pairs)))
    whole = pl.BlockSpec(memory_space=pltpu.VMEM)
    shape = jax.ShapeDtypeStruct
    in_specs = [
        pl.BlockSpec(memory_space=pltpu.SMEM),
        pl.BlockSpec((1, 2, WINDOW), lambda i: (lax.rem(i, pairs), 0, 0)),
        cols(block + GP),
        cols(ext),
        cols(ext),
        cols(GP),
        cols(GP),
        cols(block),
        cols(block),
        whole,
        cols(GP),
        whole,
    ]
    rows = block + quarter
    outs = [shape((rows, width), BF16)] * 3 + [shape((pairs, 2, WINDOW), F32)]
    others = seq_count - 1
    scratch = [
        pltpu.VMEM((pairs, ext, PAIR), F32),
        pltpu.VMEM((pairs, ext, PAIR), F32),
        pltpu.VMEM((pairs, GP, PAIR), F32),
        pltpu.VMEM((pairs, GP, PAIR), F32),
        pltpu.VMEM((seq_count, pairs, quarter, PAIR), BF16),
        pltpu.VMEM((others, pairs, quarter, PAIR), BF16),
        pltpu.VMEM((seq_count, pairs, quarter, 2 * PAIR), BF16),
        pltpu.VMEM((others, pairs, quarter, 2 * PAIR), BF16),
        pltpu.VMEM((2, pairs, 2, REACH, PAIR), BF16),
        pltpu.VMEM((2, pairs, 2, REACH, PAIR), BF16),
        pltpu.SemaphoreType.DMA((2, others, pairs)),
        pltpu.SemaphoreType.DMA((2, others, pairs)),
        pltpu.SemaphoreType.DMA((2, pairs)),
        pltpu.SemaphoreType.DMA((2, pairs)),
    ]
    args = [doc_len, table, q, kx, vx, kg, vg, o, do, l, dog, ldg]
    if early_rows:
        in_specs.append(pl.BlockSpec(memory_space=pl.ANY))
        outs.append(shape((early_rows, width), F32))
        scratch += Reducer.scratch(early_rows, width, 1)
        args.append(pieces)
    return pl.pallas_call(
        functools.partial(back_kernel, sizes, early_rows),
        grid=(2 * pairs,),
        in_specs=in_specs,
        out_specs=[whole] * len(outs),
        out_shape=outs,
        scratch_shapes=scratch,
        compiler_params=pltpu.CompilerParams(
            collective_id=1, has_side_effects=True, vmem_limit_bytes=60 * 2**20
        ),
        name="attend_back",
    )(*args)


def on_device(
    long_input,
    global_input,
    lengths,
    w_query,
    b_query,
    w_key,
    w_value,
    b_value,
    w_out,
    b_out,
    w_inner,
    b_inner,
    w_outer,
    b_outer,
    norm1_gain,
    norm1_shift,
    norm2_gain,
    norm2_shift,
    rel_table,
    long_cotangent,
    global_cotangent,
):
    seq_count = lax.axis_size("seq")
    data_count = lax.axis_size("dp")
    seq_index = lax.axis_index("seq")
    block = long_input.shape[1]
    count = global_input.shape[1]
    width = long_input.shape[2]
    heads = rel_table.shape[1]
    pairs = heads // 2
    labels = 2 * R + 1
    quarter = GP // seq_count
    sizes = Sizes(block, count, quarter, seq_count, pairs)
    queries, kx, vx, kg, vg, attn_low, long_l, glob_l, glob_x, table = attend(
        sizes,
        lengths,
        rel_table,
        long_input[0],
        global_input[0],
        w_query,
        w_key,
        w_value,
        b_query,
        b_value,
        norm1_gain,
        norm1_shift,
    )
    planned = has_plan()
    long_result, glob_out, grad_mid, grad_attn, every_do, every_ld, *gradients = feed_forward(
        sizes,
        planned,
        lengths,
        attn_low,
        long_input[0],
        glob_x,
        long_cotangent[0],
        global_cotangent[0],
        glob_l,
        w_out,
        b_out,
        norm2_gain,
        norm2_shift,
        w_inner,
        b_inner,
        w_outer,
        b_outer,
    )
    query_low, key_low, value_low, dtab, *early = attend_back(
        sizes,
        lengths,
        table,
        queries,
        kx,
        vx,
        kg,
        vg,
        attn_low,
        grad_attn,
        long_l,
        every_do,
        every_ld,
        *(gradients[:1] if planned else []),
    )
    long_grad, glob_grad, *late, sums = last_part(
        sizes,
        planned,
        long_input[0],
        glob_x,
        query_low,
        key_low,
        value_low,
        grad_mid,
        w_query,
        w_key,
        w_value,
        norm1_gain,
        norm1_shift,
        dtab,
    )
    if planned:
        (
            g_query,
            g_key,
            g_value,
            g_out,
            g_inner,
            g_outer,
            g_b_query,
            g_b_value,
            g_b_out,
            g_b_outer,
            g_g1,
            g_s1,
            g_g2,
            g_s2,
            g_b_inner,
            table_total,
        ) = small_results(heads, early[0], late[0], gradients[1], gradients[2], sums)
    else:
        devices = data_count * seq_count
        own_part = lambda vector: lax.dynamic_slice_in_dim(
            vector,
            (lax.axis_index("dp") * seq_count + seq_index) * (vector.shape[0] // devices),
            vector.shape[0] // devices,
        )
        g_outer, g_inner, g_out, vectors = gradients
        g_outer, g_inner, g_out, g_query, g_key, g_value = (
            lax.psum_scatter(g.astype(BF16), ("dp", "seq"), scatter_dimension=0, tiled=True).astype(
                F32
            )
            for g in (g_outer, g_inner, g_out, *late)
        )
        vectors, sums = lax.psum((vectors, sums), ("dp", "seq"))
        g_b_query, g_b_value, g_g1, g_s1 = (own_part(sums[heads + i]) for i in range(4))
        g_b_out, g_b_outer, g_g2, g_s2 = (own_part(vectors[i]) for i in range(4))
        g_b_inner = own_part(vectors[4:].reshape(-1))
        table_total = sums[:heads, HALO - R : HALO - R + labels].T
    return (
        long_result[None],
        glob_out[None],
        long_grad[None],
        glob_grad[None],
        g_query,
        g_b_query,
        g_key,
        g_value,
        g_b_value,
        g_out,
        g_b_out,
        g_inner,
        g_b_inner,
        g_outer,
        g_b_outer,
        g_g1,
        g_s1,
        g_g2,
        g_s2,
        table_total,
    )


def solution(mesh):
    rows, whole = P("dp", "seq", None), P("dp", None, None)
    matrix, vector = P(("dp", "seq"), None), P(("dp", "seq"))
    return jax.shard_map(
        on_device,
        mesh=mesh,
        in_specs=(rows, whole, P("dp")) + (P(),) * 16 + (rows, whole),
        out_specs=(
            rows,
            whole,
            rows,
            whole,
            matrix,
            vector,
            matrix,
            matrix,
            vector,
            matrix,
            vector,
            matrix,
            vector,
            matrix,
            vector,
            vector,
            vector,
            vector,
            vector,
            P(),
        ),
        check_vma=False,
    )
```

profile of v0, /device:TPU:0, one launch (start us, length us, event | category | flops | bytes accessed | tf_op | source)
XLA Modules:
  0.0 202.1 jit_solution(6950345870687026670)
XLA Ops:
  1.3 1.5 copy.41.rel_ref
  2.8 29.4 %attend.1 = (bf16[768,768]{1,0:T(8,128)(2,1)}, bf16[768,768]{1,0:T(8,128)(2,1)}, bf16[768,768]{1,0:T(8,128)(2,1)}, bf16[256,768]{1,0:T(8,128)(2,1)}, bf16[256,76...) custom-call(s32[1]{0:T(128)S(6)} %copy.47.len_ref, ...), custom_call_target="tpu_custom_call" | custom-call | tf_op jit(solution)/shard_map/attend/pallas_call | solution.py:345
  32.2 70.9 %feed_forward.1 = (bf16[512,768]{1,0:T(8,128)(2,1)}, bf16[230,768]{1,0:T(8,128)(2,1)}, f32[576,768]{1,0:T(8,128)}, bf16[576,768]{1,0:T(8,128)(2,1)}, bf16[256,76...) custom-call(s32[1]{0:T(128)S(6)} %copy.47.len_ref, ...), custom_call_target="tpu_custom_call" | custom-call | tf_op jit(solution)/shard_map/feed_forward/pallas_call | solution.py:1176
  103.1 45.6 %attend_back.1 = (bf16[576,768]{1,0:T(8,128)(2,1)}, bf16[576,768]{1,0:T(8,128)(2,1)}, bf16[576,768]{1,0:T(8,128)(2,1)}, f32[6,2,512]{2,1,0:T(2,128)}, f32[80,768]{1,0:T(8,128)}) custom-call(s32[1]{0:T(128)S(6)} %copy.47.len_ref, f32[6,2,512]{2,1,0:T(2,128)} %get-tuple-element.69.tab_ref, bf16[768,768]{1,0:T(8,128)(2,1)} %get-tuple-element.70.q_ref, ...), custom_call_target="tpu_custom_call" | custom-call | tf_op jit(solution)/shard_map/attend_back/pallas_call | solution.py:1504
  148.7 43.8 %last_part.1 = (f32[512,768]{1,0:T(8,128)}, f32[230,768]{1,0:T(8,128)}, f32[80,768]{1,0:T(8,128)}, f32[16,768]{1,0:T(8,128)}) custom-call(bf16[512,768]{1,0:T(8,128)(2,1)} %bitcast.10, bf16[256,768]{1,0:T(8,128)(2,1)} %get-tuple-element.65.glob_ref, bf16[576,768]{1,0:T(8,128)(2,1)} %get-tuple-element.80.dq_ref, bf16[576,768]{1,0:T(8,128)(2,1)} %get-tuple-element.81.dk_ref, ...), custom_call_target="tpu_custom_call" | custom-call | tf_op jit(solution)/shard_map/last_part/pallas_call | solution.py:776
  192.4 0.0 copy-start.1
  192.4 2.8 %copy.42 = f32[1,230,768]{2,0,1:T(1,128)} copy(f32[1,230,768]{2,1,0:T(8,128)} %bitcast.14) | data formatting | bytes 1413120
  195.2 0.0 copy-start.2
  195.2 2.4 %small_results.1 = (f32[24,768]{1,0:T(8,128)}, f32[24,768]{1,0:T(8,128)}, f32[24,768]{1,0:T(8,128)}, f32[24,768]{1,0:T(8,128)}, f32[24,3072]{1,0:T(8,128)}, /*in...) custom-call(f32[80,768]{1,0:T(8,128)} %get-tuple-element.87.early_re, ...), custom_call_target="tpu_custom_call" | custom-call | tf_op jit(solution)/shard_map/small_results/pallas_call | solution.py:830
  197.6 0.0 copy-start
  197.6 1.7 copy.43
  199.3 0.0 copy-done.1
  199.3 0.9 copy.48
  200.2 0.0 copy-done.2
  200.2 0.7 copy.49
  200.9 0.0 copy-done
  201.0 1.1 copy.50
Async XLA Ops:
  192.4 6.9 %copy-start.1 = (bf16[512,768]{1,0:T(8,128)(2,1)S(1)}, bf16[512,768]{1,0:T(8,128)(2,1)}, u32[]{:S(2)}) copy-start(bf16[512,768]{1,0:T(8,128)(2,1)} %get-tuple-element.67) | copy-start | bytes 2359300
  195.2 5.0 %copy-start.2 = (bf16[230,768]{1,0:T(8,128)(2,1)S(1)}, bf16[230,768]{1,0:T(8,128)(2,1)}, u32[]{:S(2)}) copy-start(bf16[230,768]{1,0:T(8,128)(2,1)} %get-tuple-element.68) | copy-start | bytes 1059844
  197.6 3.3 %copy-start = (f32[512,768]{1,0:T(8,128)S(1)}, f32[512,768]{1,0:T(8,128)}, u32[]{:S(2)}) copy-start(f32[512,768]{1,0:T(8,128)} %get-tuple-element.85) | copy-start | bytes 4718596
where the time goes:
time: 202 us
  Pallas kernels  192 us (95%)
  local copies, waits for them, and re-layouts  8.68 us (4%)
    pallas_call x1, Pallas kernels, feed_forward(): pl.pallas_call(functools.partial(ffn_kernel, sizes, planned), grid=(4,),...  70.9 us
    pallas_call x1, Pallas kernels, attend_back(): pl.pallas_call(functools.partial(back_kernel, sizes, early_rows), grid=(2...  45.6 us
    pallas_call x1, Pallas kernels, last_part(): pl.pallas_call(functools.partial(late_kernel, sizes, planned), in_specs=[...  43.8 us
    pallas_call x1, Pallas kernels, attend(): pl.pallas_call(functools.partial(attend_kernel, sizes), in_specs=[pl.Bloc...  29.4 us
    unnamed x12, local copies, waits for them, and re-layouts  8.68 us

commit v1 on v0

--- a/solution.py
+++ b/solution.py
@@ -378,27 +378,36 @@
 
 
 class Reducer:
-    def __init__(self, rows, split, scratch, pieces=None, order=None):
+    def __init__(self, rows, split, scratch, pieces=None, order=None, parts=None):
         self.ids = mesh_ids()
+        self.parts = parts
         self.order = order
         self.halves = (slice(0, split), slice(split, rows))
-        held, self.from_core, self.from_one, self.from_two, self.from_z = scratch[:5]
-        self.local, self.sends, self.recvs = scratch[5:]
+        held, self.from_core, self.from_one, self.from_two = scratch[:4]
+        self.local, self.sends, self.recvs = scratch[4:7]
+        if parts is None:
+            self.from_z, self.z_sends, self.z_recvs = scratch[7:]
         self.pieces, self.held = pieces, held
         self.mine = held.at[self.ids[3]] if pieces is None else held.at[0]
 
     @staticmethod
-    def scratch(rows, width, sides):
-        return [
+    def scratch(rows, width, sides, with_z=False):
+        buffers = [
             pltpu.VMEM((sides, 4, 2, 2, rows, width), BF16),
             pltpu.VMEM((4, 2, 2, rows, width), BF16),
             pltpu.VMEM((4, 2, rows, width), BF16),
             pltpu.VMEM((4, rows, width), BF16),
-            pltpu.VMEM((3, rows, width), BF16),
             pltpu.SemaphoreType.DMA((4,)),
-            pltpu.SemaphoreType.DMA((6, 4)),
-            pltpu.SemaphoreType.DMA((6, 4)),
+            pltpu.SemaphoreType.DMA((5, 4)),
+            pltpu.SemaphoreType.DMA((5, 4)),
         ]
+        if with_z:
+            buffers += [
+                pltpu.VMEM((3, rows, width), BF16),
+                pltpu.SemaphoreType.DMA((4,)),
+                pltpu.SemaphoreType.DMA((3,)),
+            ]
+        return buffers
 
     def partners(self):
         z, y, x, core = self.ids
@@ -482,19 +491,24 @@
         z, y, x, core = self.ids
         to = self.target(chunk)
         slot = lax.rem(z - to + 4, 4) - 1
-        return self.remote(
-            self.mine.at[to, y, x],
-            self.from_z.at[slot],
-            5,
-            chunk,
-            slot,
-            (to * 2 + y, x * 2 + core),
+        return pltpu.make_async_remote_copy(
+            src_ref=self.mine.at[to, y, x],
+            dst_ref=self.from_z.at[slot],
+            send_sem=self.z_sends.at[chunk],
+            recv_sem=self.z_recvs.at[slot],
+            device_id=(to * 2 + y, x * 2 + core),
+            device_id_type=pl.DeviceIdType.MESH,
         )
 
     def arrival(self, slot):
         z, y, x, core = self.ids
-        return self.remote(
-            self.mine.at[z, y, x], self.from_z.at[slot], 5, slot, slot, self.partners()[3]
+        return pltpu.make_async_remote_copy(
+            src_ref=self.mine.at[z, y, x],
+            dst_ref=self.from_z.at[slot],
+            send_sem=self.z_sends.at[slot],
+            recv_sem=self.z_recvs.at[slot],
+            device_id=self.partners()[3],
+            device_id_type=pl.DeviceIdType.MESH,
         )
 
     def leaves(self, chunk):
@@ -544,27 +558,80 @@
         to = self.target(chunk)
         for copy in self.second_copies(chunk):
             copy.wait_recv()
+        if self.parts is not None:
+            self.parts[to] = self.mine[to, y, x] + self.from_two[to]
+            return
 
         @pl.when(self.leaves(chunk))
         def _():
             self.mine[to, y, x] = self.mine[to, y, x] + self.from_two[to]
             self.last_copy(chunk).start()
 
-    def finish(self, out):
+    def finish(self, out=None):
         z, y, x, core = self.ids
-        total = self.mine[z, y, x].astype(F32) + self.from_two[z].astype(F32)
-        for slot in range(3):
-            self.arrival(slot).wait_recv()
-            total += self.from_z[slot].astype(F32)
-        out[...] = total
+        if self.parts is None:
+            total = self.mine[z, y, x].astype(F32) + self.from_two[z].astype(F32)
+            for slot in range(3):
+                self.arrival(slot).wait_recv()
+                total += self.from_z[slot].astype(F32)
+            out[...] = total
         for chunk in range(4):
             self.core_copy(chunk).wait_send()
             for copy in self.first_copies(chunk) + self.second_copies(chunk):
                 copy.wait_send()
-
-            @pl.when(self.leaves(chunk))
-            def _(chunk=chunk):
-                self.last_copy(chunk).wait_send()
+            if self.parts is None:
+
+                @pl.when(self.leaves(chunk))
+                def _(chunk=chunk):
+                    self.last_copy(chunk).wait_send()
+
+
+class ZSum:
+    def __init__(self, parts, scratch):
+        self.ids = mesh_ids()
+        self.parts = parts
+        self.own, self.from_z, self.local, self.sends, self.recvs = scratch
+
+    @staticmethod
+    def scratch(rows, width):
+        return [
+            pltpu.VMEM((rows, width), BF16),
+            pltpu.VMEM((3, rows, width), BF16),
+            pltpu.SemaphoreType.DMA,
+            pltpu.SemaphoreType.DMA((3,)),
+            pltpu.SemaphoreType.DMA((3,)),
+        ]
+
+    def own_copy(self):
+        return pltpu.make_async_copy(self.parts.at[self.ids[0]], self.own, self.local)
+
+    def copies(self):
+        z, y, x, core = self.ids
+        for slot in range(3):
+            to = lax.rem(z + 3 - slot, 4)
+            yield pltpu.make_async_remote_copy(
+                src_ref=self.parts.at[to],
+                dst_ref=self.from_z.at[slot],
+                send_sem=self.sends.at[slot],
+                recv_sem=self.recvs.at[slot],
+                device_id=(to * 2 + y, x * 2 + core),
+                device_id_type=pl.DeviceIdType.MESH,
+            )
+
+    def start(self):
+        self.own_copy().start()
+        for copy in self.copies():
+            copy.start()
+
+    def finish(self, out):
+        self.own_copy().wait()
+        total = self.own[...].astype(F32)
+        for slot, copy in enumerate(self.copies()):
+            copy.wait_recv()
+            total += self.from_z[slot].astype(F32)
+        out[...] = total
+        for copy in self.copies():
+            copy.wait_send()
 
 
 def mesh_ids():
@@ -610,17 +677,15 @@
     gain_ref,
     shift_ref,
     table_ref,
-    long_out,
-    glob_out,
     *rest,
 ):
     block, count, quarter, seq_count, pairs = sizes
     rows = block + quarter
     width = long_ref.shape[1]
     if planned:
-        late_ref, total_ref, *rest = rest
+        early_parts, long_out, glob_out, late_ref, total_ref, early_ref, *rest = rest
     else:
-        gq_ref, gk_ref, gv_ref, total_ref, *rest = rest
+        long_out, glob_out, gq_ref, gk_ref, gv_ref, total_ref, *rest = rest
     normed_t, every, gather_sends, gather_recvs, *rest = rest
     seq_index = lax.axis_index("seq")
     own_rows = pl.ds(pl.multiple_of(seq_index * quarter, quarter), quarter)
@@ -639,7 +704,8 @@
 
     if planned:
         kept, arrived, table_sends, table_recvs, *rest = rest
-        reducer = Reducer(rest[0].shape[-2], 32, rest)
+        z_sum = ZSum(early_parts, rest[:5])
+        reducer = Reducer(rest[5].shape[-2], 32, rest[5:])
         z, y, x, core = mesh_ids()
         partners = reducer.partners()[:3] + [
             ((z + 1 - 2 * lax.rem(z, 2)) * 2 + y, lax.axis_index("seq")),
@@ -663,6 +729,8 @@
                 table_copy(stage + 1).start()
 
     meet(others + (reducer.partners()[2:] if planned else []))
+    if planned:
+        z_sum.start()
     everything = jnp.concatenate([long_ref[...], glob_ref[own_rows]], 0).astype(F32)
     hat, inverse = row_norm(everything)
     normed_t[...] = (hat * gain_ref[...] + shift_ref[...]).astype(BF16).T
@@ -728,6 +796,7 @@
             getattr(reducer, act)(chunk)
             table_step(number)
         total_ref[...] = kept[5]
+        z_sum.finish(early_ref)
         reducer.finish(late_ref)
         for stage in range(5):
             table_copy(stage).wait_send()
@@ -747,7 +816,7 @@
 )
 
 
-def last_part(sizes, planned, long_x, glob_x, dq, dk, dv, dmid, wq, wk, wv, gain, shift, table):
+def last_part(sizes, planned, long_x, glob_x, dq, dk, dv, dmid, *weights):
     block, count, quarter, seq_count, pairs = sizes
     rows, width = dq.shape
     others = seq_count - 1
@@ -764,18 +833,20 @@
     if planned:
         piece = width // 32
         part = 3 * piece + 8
-        outs += [shape((part, width), F32), sums]
+        early = weights[-1].shape[1:]
+        outs += [shape((part, width), F32), sums, shape(early, F32)]
         scratch += [
             pltpu.VMEM((6,) + sums.shape, F32),
             pltpu.VMEM((5,) + sums.shape, F32),
             pltpu.SemaphoreType.DMA((5,)),
             pltpu.SemaphoreType.DMA((5,)),
-        ] + Reducer.scratch(part, width, 2)
+        ]
+        scratch += ZSum.scratch(*early) + Reducer.scratch(part, width, 2, with_z=True)
     else:
         outs += [shape((width, width), BF16)] * 3 + [sums]
     return pl.pallas_call(
         functools.partial(late_kernel, sizes, planned),
-        in_specs=[whole] * 12,
+        in_specs=[whole] * 12 + [pl.BlockSpec(memory_space=pl.ANY)] * planned,
         out_specs=[whole] * len(outs),
         out_shape=outs,
         scratch_shapes=scratch,
@@ -783,10 +854,19 @@
             collective_id=2, has_side_effects=True, vmem_limit_bytes=60 * 2**20
         ),
         name="last_part",
-    )(long_x, glob_x, dq, dk, dv, dmid, wq, wk, wv, gain, shift, table)
-
-
-def small_kernel(heads, early_ref, late_ref, outer_ref, inner_ref, sums_ref, *outs):
+    )(long_x, glob_x, dq, dk, dv, dmid, *weights)
+
+
+def small_kernel(heads, early_ref, late_ref, outer_ref, inner_ref, sums_ref, *rest):
+    *refs, sems = rest
+    big = len(refs) - 16
+    outs = refs[big // 2 : big // 2 + 16]
+    copies = [
+        pltpu.make_async_copy(source, dest, sems.at[at])
+        for at, (source, dest) in enumerate(zip(refs, refs[big // 2 + 16 :]))
+    ]
+    for copy in copies:
+        copy.start()
     g_query, g_key, g_value, g_out, g_inner, g_outer, *vectors, table = outs
     device = lax.axis_index("dp") * lax.axis_size("seq") + lax.axis_index("seq")
     piece, width = g_query.shape
@@ -816,9 +896,11 @@
     labels = table.shape[0]
     turned = pltpu.roll(sums_ref[:, :WINDOW], WINDOW - HALO + R, 1).T
     table[...] = turned[:labels, :heads]
-
-
-def small_results(heads, early, late, outer, inner, sums):
+    for copy in copies:
+        copy.wait()
+
+
+def small_results(heads, early, late, outer, inner, sums, *big):
     width = early.shape[1]
     piece = width // 32
     shape = jax.ShapeDtypeStruct
@@ -827,13 +909,15 @@
     outs += [shape((piece, 4 * width), F32), shape((4 * piece, width), F32)]
     outs += [shape((piece,), F32)] * 8 + [shape((4 * piece,), F32)]
     outs += [shape((2 * R + 1, heads), F32)]
+    there = [pl.BlockSpec(memory_space=pl.ANY)] * len(big)
     return pl.pallas_call(
         functools.partial(small_kernel, heads),
-        in_specs=[whole] * 5,
-        out_specs=[whole] * len(outs),
-        out_shape=outs,
+        in_specs=[whole] * 5 + there,
+        out_specs=[whole] * len(outs) + there,
+        out_shape=outs + [shape(part.shape, part.dtype) for part in big],
+        scratch_shapes=[pltpu.SemaphoreType.DMA((len(big),))],
         name="small_results",
-    )(early, late, outer, inner, sums)
+    )(early, late, outer, inner, sums, *big)
 
 
 def has_plan():
@@ -900,15 +984,14 @@
         biases,
         every_do,
         every_ld,
-        every_out,
         gather_sends,
         gather_recvs,
         *rest,
     ) = rest
     if planned:
         even, *rest = rest
-        outer = Reducer(rest[0].shape[-2], 48, rest[:8], order=chunk_of)
-        inner = Reducer(rest[8].shape[-2], 16, rest[8:])
+        outer = Reducer(rest[0].shape[-2], 48, rest[:7], order=chunk_of, parts=outer_ref)
+        inner = Reducer(rest[7].shape[-2], 16, rest[7:], parts=inner_ref)
     step = pl.program_id(0)
     chunk = chunk_of(step)
     seq_index = lax.axis_index("seq")
@@ -916,18 +999,30 @@
     width = mid.shape[1]
     piece = width // 32
 
-    def gathers(kinds):
-        for seq_step in range(1, seq_count):
-            for kind in kinds:
-                every = (every_do, every_ld, every_out)[kind]
-                yield pltpu.make_async_remote_copy(
-                    src_ref=every.at[own_rows],
-                    dst_ref=every.at[own_rows],
-                    send_sem=gather_sends.at[kind, seq_step - 1],
-                    recv_sem=gather_recvs.at[kind, seq_step - 1],
-                    device_id=seq_device(seq_step, seq_count),
-                    device_id_type=pl.DeviceIdType.MESH,
-                )
+    def rows_of(device):
+        return pl.ds(pl.multiple_of(device[1] * quarter, quarter), quarter)
+
+    def gather(owner, device, at):
+        for kind, every in enumerate((every_do, every_ld)):
+            yield pltpu.make_async_remote_copy(
+                src_ref=every.at[rows_of(owner)],
+                dst_ref=every.at[rows_of(owner)],
+                send_sem=gather_sends.at[kind, at],
+                recv_sem=gather_recvs.at[kind, at],
+                device_id=device,
+                device_id_type=pl.DeviceIdType.MESH,
+            )
+
+    me = seq_device(0, seq_count)
+    if planned:
+        sibling, across = outer.partners()[:2]
+        first_gathers = [(me, across, 0), (me, sibling, 1)]
+        second_gathers = [(across, sibling, 2)]
+    else:
+        first_gathers = [
+            (me, seq_device(at + 1, seq_count), at) for at in range(seq_count - 1)
+        ]
+        second_gathers = []
 
     def act(now):
         if planned:
@@ -1042,15 +1137,21 @@
             delta = jnp.sum(own_half(head % 2, both[:, lanes]), -1, keepdims=True)
             stats = jnp.where(lane_index() == HD + head, delta, stats)
         every_ld[own_rows] = stats
-        every_out[own_rows] = y_sum[block:].astype(BF16)
-        for copy in gathers((0, 1, 2)):
-            copy.start()
+        for part in first_gathers:
+            for copy in gather(*part):
+                copy.start()
+        glob_out[...] = y_sum[block:].astype(BF16)
         act((4, 0))
         position = seq_index * block + lax.broadcasted_iota(jnp.int32, (block, 1), 0)
         long_out[...] = jnp.where(position < len_ref[0], y_sum[:block], 0.0).astype(BF16)
         long_sums, long_low, _ = norm_back(slice(0, block))
         for at, one, two in zip((0, 2, 3), long_sums, glob_sums):
             vectors[at : at + 1] = one + two
+        if planned:
+            for copy in gather(*first_gathers[0]):
+                copy.wait_recv()
+            for copy in gather(*second_gathers[0]):
+                copy.start()
         act((4, 1))
         g_out = t_dot(attn_ref[...], jnp.concatenate([long_low, glob_low], 0))
         if planned:
@@ -1061,18 +1162,19 @@
                     ).astype(BF16)
                 )
             act((4, 2))
-            outer.finish(outer_ref)
-            inner.finish(inner_ref)
+            outer.finish()
+            inner.finish()
         else:
             g_out_ref[...] = g_out.astype(BF16)
             vec_ref[...] = vectors[...]
-        for copy in gathers((0, 1, 2)):
-            copy.wait_recv()
+        for part in (first_gathers[1:] if planned else first_gathers) + second_gathers:
+            for copy in gather(*part):
+                copy.wait_recv()
         dog_ref[...] = every_do[...]
         ldg_ref[...] = every_ld[...]
-        glob_out[...] = every_out[:count]
-        for copy in gathers((0, 1, 2)):
-            copy.wait_send()
+        for part in first_gathers + second_gathers:
+            for copy in gather(*part):
+                copy.wait_send()
 
 
 OUTER, INNER = 0, 1
@@ -1125,7 +1227,7 @@
     ]
     outs = [
         shape((block, width), BF16),
-        shape((count, width), BF16),
+        shape((quarter, width), BF16),
         shape((rows, width), F32),
         shape((rows, width), BF16),
         shape((GP, width), BF16),
@@ -1144,16 +1246,15 @@
         pltpu.VMEM((4, 1, chunk), F32),
         pltpu.VMEM((GP, width), BF16),
         pltpu.VMEM((GP, PAIR), F32),
-        pltpu.VMEM((GP, width), BF16),
-        pltpu.SemaphoreType.DMA((3, others)),
-        pltpu.SemaphoreType.DMA((3, others)),
+        pltpu.SemaphoreType.DMA((2, others)),
+        pltpu.SemaphoreType.DMA((2, others)),
     ]
     if planned:
         part, piece = hidden // 32, width // 32
         outs += [
             shape((2, 4, 2, 2, 3 * piece + 8, width), BF16),
-            shape((part, width), F32),
-            shape((2 * piece, width), F32),
+            shape((4, part, width), BF16),
+            shape((4, 2 * piece, width), BF16),
         ]
         out_specs += [whole] * 3
         scratch += [
@@ -1202,15 +1303,16 @@
     l_ref,
     dog_ref,
     ldg_ref,
+    yq_ref,
     *rest,
 ):
     block, count, quarter, seq_count, pairs = sizes
     reduces = early_rows > 0
     if reduces:
-        pieces_ref, rest = rest[0], rest[1:]
-    dq_ref, dk_ref, dv_ref, dtab_ref, *rest = rest
+        pieces_ref, outer_parts, inner_parts, *rest = rest
+    dq_ref, dk_ref, dv_ref, dtab_ref, glob_out, *rest = rest
     if reduces:
-        early_ref, rest = rest[0], rest[1:]
+        early_parts, outer_ref, inner_ref, *rest = rest
     (
         dkx,
         dvx,
@@ -1226,12 +1328,20 @@
         glob_recvs,
         halo_sends,
         halo_recvs,
+        every,
+        gather_sends,
+        gather_recvs,
         *rest,
     ) = rest
     number = pl.program_id(0)
     pair = lax.rem(number, pairs)
     seq_index = lax.axis_index("seq")
-    reducer = Reducer(early_rows, 16, rest, pieces=pieces_ref) if reduces else None
+    if reduces:
+        reducer = Reducer(early_rows, 16, rest[:7], pieces=pieces_ref, parts=early_parts)
+        z_sums = (
+            (ZSum(outer_parts, rest[7:12]), outer_ref),
+            (ZSum(inner_parts, rest[12:]), inner_ref),
+        )
     scale = HD ** (-0.5)
     low_lanes = lane_index() < HD
     own_keys = slice(HALO, HALO + block)
@@ -1247,6 +1357,17 @@
                 send_sem=glob_sends.at[kind, step - 1, at],
                 recv_sem=glob_recvs.at[kind, step - 1, at],
                 device_id=device,
+                device_id_type=pl.DeviceIdType.MESH,
+            )
+
+    def gathers():
+        for step in range(1, seq_count):
+            yield pltpu.make_async_remote_copy(
+                src_ref=every.at[own_rows],
+                dst_ref=every.at[own_rows],
+                send_sem=gather_sends.at[step - 1],
+                recv_sem=gather_recvs.at[step - 1],
+                device_id=seq_device(step, seq_count),
                 device_id_type=pl.DeviceIdType.MESH,
             )
 
@@ -1304,6 +1425,11 @@
         if reduces:
             for chunk in range(4):
                 reducer.start(chunk)
+            for z_sum, _ in z_sums:
+                z_sum.start()
+        every[own_rows] = yq_ref[...]
+        for copy in gathers():
+            copy.start()
         for direction in range(2):
 
             @pl.when(jnp.logical_not(gets_from[direction]))
@@ -1450,14 +1576,21 @@
                 def _(direction=direction, at=at):
                     halo_copy(direction, at).wait_send()
 
+        for copy in gathers():
+            copy.wait_recv()
+        glob_out[...] = every[:count]
+        for copy in gathers():
+            copy.wait_send()
         if reduces:
-            reducer.finish(early_ref)
-
-
-def attend_back(sizes, doc_len, table, q, kx, vx, kg, vg, o, do, l, dog, ldg, pieces=None):
+            reducer.finish()
+            for z_sum, out in z_sums:
+                z_sum.finish(out)
+
+
+def attend_back(sizes, doc_len, table, q, kx, vx, kg, vg, o, do, l, dog, ldg, yq, *sums):
     block, count, quarter, seq_count, pairs = sizes
     width = q.shape[1]
-    early_rows = 0 if pieces is None else pieces.shape[-2]
+    early_rows = sums[0].shape[-2] if sums else 0
     ext = block + 2 * HALO
     cols = lambda rows: pl.BlockSpec((rows, PAIR), lambda i: (0, lax.rem(i, pairs)))
     whole = pl.BlockSpec(memory_space=pltpu.VMEM)
@@ -1475,9 +1608,11 @@
         whole,
         cols(GP),
         whole,
+        whole,
     ]
     rows = block + quarter
     outs = [shape((rows, width), BF16)] * 3 + [shape((pairs, 2, WINDOW), F32)]
+    outs.append(shape((count, width), BF16))
     others = seq_count - 1
     scratch = [
         pltpu.VMEM((pairs, ext, PAIR), F32),
@@ -1494,13 +1629,18 @@
         pltpu.SemaphoreType.DMA((2, others, pairs)),
         pltpu.SemaphoreType.DMA((2, pairs)),
         pltpu.SemaphoreType.DMA((2, pairs)),
+        pltpu.VMEM((GP, width), BF16),
+        pltpu.SemaphoreType.DMA((others,)),
+        pltpu.SemaphoreType.DMA((others,)),
     ]
-    args = [doc_len, table, q, kx, vx, kg, vg, o, do, l, dog, ldg]
+    args = [doc_len, table, q, kx, vx, kg, vg, o, do, l, dog, ldg, yq, *sums]
     if early_rows:
-        in_specs.append(pl.BlockSpec(memory_space=pl.ANY))
-        outs.append(shape((early_rows, width), F32))
+        in_specs += [pl.BlockSpec(memory_space=pl.ANY)] * 3
+        outs.append(shape((4, early_rows, width), BF16))
         scratch += Reducer.scratch(early_rows, width, 1)
-        args.append(pieces)
+        for parts in sums[1:]:
+            outs.append(shape(parts.shape[1:], F32))
+            scratch += ZSum.scratch(*parts.shape[1:])
     return pl.pallas_call(
         functools.partial(back_kernel, sizes, early_rows),
         grid=(2 * pairs,),
@@ -1564,7 +1704,7 @@
         norm1_shift,
     )
     planned = has_plan()
-    long_result, glob_out, grad_mid, grad_attn, every_do, every_ld, *gradients = feed_forward(
+    long_result, own_out, grad_mid, grad_attn, every_do, every_ld, *gradients = feed_forward(
         sizes,
         planned,
         lengths,
@@ -1583,7 +1723,7 @@
         w_outer,
         b_outer,
     )
-    query_low, key_low, value_low, dtab, *early = attend_back(
+    query_low, key_low, value_low, dtab, glob_out, *early = attend_back(
         sizes,
         lengths,
         table,
@@ -1597,9 +1737,10 @@
         long_l,
         every_do,
         every_ld,
-        *(gradients[:1] if planned else []),
+        own_out,
+        *(gradients if planned else []),
     )
-    long_grad, glob_grad, *late, sums = last_part(
+    long_grad, glob_grad, *late = last_part(
         sizes,
         planned,
         long_input[0],
@@ -1614,6 +1755,7 @@
         norm1_gain,
         norm1_shift,
         dtab,
+        *early[:1],
     )
     if planned:
         (
@@ -1633,7 +1775,11 @@
             g_s2,
             g_b_inner,
             table_total,
-        ) = small_results(heads, early[0], late[0], gradients[1], gradients[2], sums)
+            long_grad,
+            long_result,
+        ) = small_results(
+            heads, late[2], late[0], early[1], early[2], late[1], long_grad, long_result
+        )
     else:
         devices = data_count * seq_count
         own_part = lambda vector: lax.dynamic_slice_in_dim(
@@ -1646,9 +1792,9 @@
             lax.psum_scatter(g.astype(BF16), ("dp", "seq"), scatter_dimension=0, tiled=True).astype(
                 F32
             )
-            for g in (g_outer, g_inner, g_out, *late)
+            for g in (g_outer, g_inner, g_out, *late[:3])
         )
-        vectors, sums = lax.psum((vectors, sums), ("dp", "seq"))
+        vectors, sums = lax.psum((vectors, late[3]), ("dp", "seq"))
         g_b_query, g_b_value, g_g1, g_s1 = (own_part(sums[heads + i]) for i in range(4))
         g_b_out, g_b_outer, g_g2, g_s2 = (own_part(vectors[i]) for i in range(4))
         g_b_inner = own_part(vectors[4:].reshape(-1))

time: 202 us -> 261 us (1.29)
  Pallas kernels: 192 us -> 254 us
  local copies, waits for them, and re-layouts: 8.68 us -> 5.41 us
    pallas_call x1, Pallas kernels: 2.42 us -> 74.9 us  [small_results(): pl.pallas_call(functools.partial(small_kernel, heads), in_specs=[whole] *...]
    pallas_call x1, Pallas kernels: 70.9 us -> 61 us  [feed_forward(): pl.pallas_call(functools.partial(ffn_kernel, sizes, planned), grid=(4,),...]
    unnamed x12 -> x8, local copies, waits for them, and re-layouts: 8.68 us -> 5.41 us
where the time goes in v1:
time: 261 us; the launch traced here: 260 us
  Pallas kernels  254 us (97%)
  local copies, waits for them, and re-layouts  5.41 us (2%)
    pallas_call x1, Pallas kernels, small_results(): pl.pallas_call(functools.partial(small_kernel, heads), in_specs=[whole] *...  74.9 us
    pallas_call x1, Pallas kernels, feed_forward(): pl.pallas_call(functools.partial(ffn_kernel, sizes, planned), grid=(4,),...  61 us
    pallas_call x1, Pallas kernels, last_part(): pl.pallas_call(functools.partial(late_kernel, sizes, planned), in_specs=[...  45 us
    pallas_call x1, Pallas kernels, attend_back(): pl.pallas_call(functools.partial(back_kernel, sizes, early_rows), grid=(2...  43.3 us
    pallas_call x1, Pallas kernels, attend(): pl.pallas_call(functools.partial(attend_kernel, sizes), in_specs=[pl.Bloc...  29.4 us
    unnamed x8, local copies, waits for them, and re-layouts  5.41 us

profile of v1, /device:TPU:0, one launch (start us, length us, event | category | flops | bytes accessed | tf_op | source)
XLA Modules:
  0.0 260.4 jit_solution(18143004348723517416)
XLA Ops:
  1.3 1.5 copy.41.rel_ref
  2.8 29.4 %attend.1 = (bf16[768,768]{1,0:T(8,128)(2,1)}, bf16[768,768]{1,0:T(8,128)(2,1)}, bf16[768,768]{1,0:T(8,128)(2,1)}, bf16[256,768]{1,0:T(8,128)(2,1)}, bf16[256,76...) custom-call(s32[1]{0:T(128)S(6)} %copy.45.len_ref, ...), custom_call_target="tpu_custom_call" | custom-call | tf_op jit(solution)/shard_map/attend/pallas_call | solution.py:345
  32.2 61.0 %feed_forward.1 = (bf16[512,768]{1,0:T(8,128)(2,1)}, bf16[64,768]{1,0:T(8,128)(2,1)}, f32[576,768]{1,0:T(8,128)}, bf16[576,768]{1,0:T(8,128)(2,1)}, bf16[256,768...) custom-call(s32[1]{0:T(128)S(6)} %copy.45.len_ref, ...), custom_call_target="tpu_custom_call" | custom-call | tf_op jit(solution)/shard_map/feed_forward/pallas_call | solution.py:1277
  93.2 43.3 %attend_back.1 = (bf16[576,768]{1,0:T(8,128)(2,1)}, bf16[576,768]{1,0:T(8,128)(2,1)}, bf16[576,768]{1,0:T(8,128)(2,1)}, f32[6,2,512]{2,1,0:T(2,128)}, bf16[230,7...) custom-call(s32[1]{0:T(128)S(6)} %copy.45.len_ref, ...), custom_call_target="tpu_custom_call" | custom-call | tf_op jit(solution)/shard_map/attend_back/pallas_call | solution.py:1644
  136.5 45.0 %last_part.1 = (f32[512,768]{1,0:T(8,128)}, f32[230,768]{1,0:T(8,128)}, f32[80,768]{1,0:T(8,128)}, f32[16,768]{1,0:T(8,128)}, f32[80,768]{1,0:T(8,128)}) custom-call(bf16[512,768]{1,0:T(8,128)(2,1)} %bitcast.10, bf16[256,768]{1,0:T(8,128)(2,1)} %get-tuple-element.70.glob_ref, bf16[576,768]{1,0:T(8,128)(2,1)} %get-tuple-element.87.dq_ref, ...), custom_call_target="tpu_custom_call" | custom-call | tf_op jit(solution)/shard_map/last_part/pallas_call | solution.py:847
  181.5 0.0 copy-start
  181.5 74.9 %small_results.1 = (f32[24,768]{1,0:T(8,128)}, f32[24,768]{1,0:T(8,128)}, f32[24,768]{1,0:T(8,128)}, f32[24,768]{1,0:T(8,128)}, f32[24,3072]{1,0:T(8,128)}, /*in...) custom-call(f32[80,768]{1,0:T(8,128)} %get-tuple-element.93.early_re, ...), custom_call_target="tpu_custom_call" | custom-call | tf_op jit(solution)/shard_map/small_results/pallas_call | solution.py:913
  256.4 0.0 copy-start.1
  256.4 1.6 copy.43
  258.1 0.0 copy-done
  258.1 1.6 copy.42
  259.6 0.0 copy-done.1
  259.6 0.7 copy.46
Async XLA Ops:
  181.5 76.6 %copy-start = (f32[230,768]{1,0:T(8,128)S(1)}, f32[230,768]{1,0:T(8,128)}, u32[]{:S(2)}) copy-start(f32[230,768]{1,0:T(8,128)} %get-tuple-element.103) | copy-start | bytes 2119684
  256.4 3.2 %copy-start.1 = (bf16[230,768]{1,0:T(8,128)(2,1)S(1)}, bf16[230,768]{1,0:T(8,128)(2,1)}, u32[]{:S(2)}) copy-start(bf16[230,768]{1,0:T(8,128)(2,1)} %get-tuple-element.101) | copy-start | bytes 1059844

commit v2 on v1

--- a/solution.py
+++ b/solution.py
@@ -634,6 +634,72 @@
             copy.wait_send()
 
 
+class EverySum:
+    def __init__(self, scratch):
+        self.kept, self.arrived, self.from_z, self.sends, self.recvs = scratch
+        z, y, x, core = mesh_ids()
+        seq = x * 2 + core
+        self.z = z
+        self.pairs = (
+            (z * 2 + y, x * 2 + 1 - core),
+            (z * 2 + y, (1 - x) * 2 + core),
+            (z * 2 + 1 - y, seq),
+        )
+        self.along_z = [(lax.rem(z + step, 4) * 2 + y, seq) for step in (1, 2, 3)]
+
+    @staticmethod
+    def scratch(rows, width):
+        return [
+            pltpu.VMEM((3, rows, width), F32),
+            pltpu.VMEM((3, rows, width), F32),
+            pltpu.VMEM((4, rows, width), F32),
+            pltpu.SemaphoreType.DMA((6,)),
+            pltpu.SemaphoreType.DMA((6,)),
+        ]
+
+    def copy(self, stage):
+        return pltpu.make_async_remote_copy(
+            src_ref=self.kept.at[stage],
+            dst_ref=self.arrived.at[stage],
+            send_sem=self.sends.at[stage],
+            recv_sem=self.recvs.at[stage],
+            device_id=self.pairs[stage],
+            device_id_type=pl.DeviceIdType.MESH,
+        )
+
+    def z_copies(self):
+        for at, device in enumerate(self.along_z):
+            yield pltpu.make_async_remote_copy(
+                src_ref=self.from_z.at[self.z],
+                dst_ref=self.from_z.at[self.z],
+                send_sem=self.sends.at[3 + at],
+                recv_sem=self.recvs.at[3 + at],
+                device_id=device,
+                device_id_type=pl.DeviceIdType.MESH,
+            )
+
+    def step(self, stage):
+        if stage > 0:
+            self.copy(stage - 1).wait_recv()
+            total = self.kept[stage - 1] + self.arrived[stage - 1]
+            if stage < 3:
+                self.kept[stage] = total
+            else:
+                self.from_z[self.z] = total
+        if stage < 3:
+            self.copy(stage).start()
+        else:
+            for copy in self.z_copies():
+                copy.start()
+
+    def finish(self, out):
+        for copy in self.z_copies():
+            copy.wait_recv()
+        out[...] = (self.from_z[0] + self.from_z[1]) + (self.from_z[2] + self.from_z[3])
+        for copy in [self.copy(stage) for stage in range(3)] + list(self.z_copies()):
+            copy.wait_send()
+
+
 def mesh_ids():
     dp, seq = lax.axis_index("dp"), lax.axis_index("seq")
     return lax.div(dp, 2), lax.rem(dp, 2), lax.div(seq, 2), lax.rem(seq, 2)
@@ -683,9 +749,9 @@
     rows = block + quarter
     width = long_ref.shape[1]
     if planned:
-        early_parts, long_out, glob_out, late_ref, total_ref, early_ref, *rest = rest
+        early_parts, long_out, glob_out, late_ref, total_ref, scale_ref, early_ref, *rest = rest
     else:
-        long_out, glob_out, gq_ref, gk_ref, gv_ref, total_ref, *rest = rest
+        long_out, glob_out, gq_ref, gk_ref, gv_ref, total_ref, scale_ref, *rest = rest
     normed_t, every, gather_sends, gather_recvs, *rest = rest
     seq_index = lax.axis_index("seq")
     own_rows = pl.ds(pl.multiple_of(seq_index * quarter, quarter), quarter)
@@ -703,33 +769,20 @@
             )
 
     if planned:
-        kept, arrived, table_sends, table_recvs, *rest = rest
-        z_sum = ZSum(early_parts, rest[:5])
-        reducer = Reducer(rest[5].shape[-2], 32, rest[5:])
-        z, y, x, core = mesh_ids()
-        partners = reducer.partners()[:3] + [
-            ((z + 1 - 2 * lax.rem(z, 2)) * 2 + y, lax.axis_index("seq")),
-            (lax.rem(z + 2, 4) * 2 + y, lax.axis_index("seq")),
-        ]
-
-        def table_copy(stage):
-            return pltpu.make_async_remote_copy(
-                src_ref=kept.at[stage],
-                dst_ref=arrived.at[stage],
-                send_sem=table_sends.at[stage],
-                recv_sem=table_recvs.at[stage],
-                device_id=partners[stage],
-                device_id_type=pl.DeviceIdType.MESH,
-            )
-
-        def table_step(stage):
-            table_copy(stage).wait_recv()
-            kept[stage + 1] = kept[stage] + arrived[stage]
-            if stage < 4:
-                table_copy(stage + 1).start()
+        first_sum, second_sum = EverySum(rest[:5]), EverySum(rest[5:10])
+        z_sum = ZSum(early_parts, rest[10:15])
+        reducer = Reducer(rest[15].shape[-2], 32, rest[15:])
 
     meet(others + (reducer.partners()[2:] if planned else []))
+    heads = 2 * pairs
+    first = first_sum.kept.at[0] if planned else total_ref
+    first[...] = jnp.zeros(first.shape, F32)
+    for pair in range(pairs):
+        first[2 * pair : 2 * pair + 2, :WINDOW] = table_ref[pair]
+    for at, ref in enumerate((dq_ref, dv_ref)):
+        first[heads + at : heads + at + 1] = column_sum(ref[...].astype(F32))
     if planned:
+        first_sum.step(0)
         z_sum.start()
     everything = jnp.concatenate([long_ref[...], glob_ref[own_rows]], 0).astype(F32)
     hat, inverse = row_norm(everything)
@@ -749,12 +802,15 @@
             reducer.start(chunk)
 
         weight_rows(0)
+        first_sum.step(1)
         weight_rows(1)
         reducer.add_core(0)
         weight_rows(2)
+        first_sum.step(2)
         reducer.add_core(1)
         weight_rows(3)
         grads = dot_t(dq_ref[...], wq_ref[...])
+        first_sum.step(3)
         reducer.add_first(0)
         reducer.add_core(2)
         grads += dot_t(dk_ref[...], wk_ref[...]) + dot_t(dv_ref[...], wv_ref[...])
@@ -779,41 +835,29 @@
     for copy in gathers():
         copy.start()
     long_out[...] = total[:block]
-    sums = [
-        column_sum(part)
-        for part in (dq_ref[...].astype(F32), dv_ref[...].astype(F32), grads * hat, grads)
-    ]
-    heads = 2 * pairs
-    first = kept.at[0] if planned else total_ref
-    first[...] = jnp.zeros(first.shape, F32)
-    for pair in range(pairs):
-        first[2 * pair : 2 * pair + 2, :WINDOW] = table_ref[pair]
-    for at, vector in enumerate(sums):
-        first[heads + at : heads + at + 1] = vector
+    second = second_sum.kept.at[0] if planned else scale_ref
+    second[...] = jnp.zeros(second.shape, F32)
+    second[0:1] = column_sum(grads * hat)
+    second[1:2] = column_sum(grads)
     if planned:
-        table_copy(0).start()
-        for number, (act, chunk) in enumerate(LATE_TAIL):
-            getattr(reducer, act)(chunk)
-            table_step(number)
-        total_ref[...] = kept[5]
+        second_sum.step(0)
+        first_sum.finish(total_ref)
+        reducer.add_first(2)
+        second_sum.step(1)
+        reducer.add_second(1)
+        reducer.add_first(3)
+        reducer.add_second(2)
+        second_sum.step(2)
+        reducer.add_second(3)
+        second_sum.step(3)
         z_sum.finish(early_ref)
         reducer.finish(late_ref)
-        for stage in range(5):
-            table_copy(stage).wait_send()
+        second_sum.finish(scale_ref)
     for copy in gathers():
         copy.wait_recv()
     glob_out[...] = every[:count].astype(F32)
     for copy in gathers():
         copy.wait_send()
-
-
-LATE_TAIL = (
-    ("add_first", 2),
-    ("add_second", 1),
-    ("add_first", 3),
-    ("add_second", 2),
-    ("add_second", 3),
-)
 
 
 def last_part(sizes, planned, long_x, glob_x, dq, dk, dv, dmid, *weights):
@@ -822,7 +866,7 @@
     others = seq_count - 1
     whole = pl.BlockSpec(memory_space=pltpu.VMEM)
     shape = jax.ShapeDtypeStruct
-    sums = shape(((2 * pairs + 4 + 7) // 8 * 8, width), F32)
+    sums = [shape(((2 * pairs + 2 + 7) // 8 * 8, width), F32), shape((8, width), F32)]
     outs = [shape((block, width), F32), shape((count, width), F32)]
     scratch = [
         pltpu.VMEM((width, rows), BF16),
@@ -834,16 +878,12 @@
         piece = width // 32
         part = 3 * piece + 8
         early = weights[-1].shape[1:]
-        outs += [shape((part, width), F32), sums, shape(early, F32)]
-        scratch += [
-            pltpu.VMEM((6,) + sums.shape, F32),
-            pltpu.VMEM((5,) + sums.shape, F32),
-            pltpu.SemaphoreType.DMA((5,)),
-            pltpu.SemaphoreType.DMA((5,)),
-        ]
+        outs += [shape((part, width), F32), *sums, shape(early, F32)]
+        for part_sums in sums:
+            scratch += EverySum.scratch(*part_sums.shape)
         scratch += ZSum.scratch(*early) + Reducer.scratch(part, width, 2, with_z=True)
     else:
-        outs += [shape((width, width), BF16)] * 3 + [sums]
+        outs += [shape((width, width), BF16)] * 3 + sums
     return pl.pallas_call(
         functools.partial(late_kernel, sizes, planned),
         in_specs=[whole] * 12 + [pl.BlockSpec(memory_space=pl.ANY)] * planned,
@@ -857,16 +897,7 @@
     )(long_x, glob_x, dq, dk, dv, dmid, *weights)
 
 
-def small_kernel(heads, early_ref, late_ref, outer_ref, inner_ref, sums_ref, *rest):
-    *refs, sems = rest
-    big = len(refs) - 16
-    outs = refs[big // 2 : big // 2 + 16]
-    copies = [
-        pltpu.make_async_copy(source, dest, sems.at[at])
-        for at, (source, dest) in enumerate(zip(refs, refs[big // 2 + 16 :]))
-    ]
-    for copy in copies:
-        copy.start()
+def small_kernel(heads, early_ref, late_ref, outer_ref, inner_ref, sums_ref, scale_ref, *outs):
     g_query, g_key, g_value, g_out, g_inner, g_outer, *vectors, table = outs
     device = lax.axis_index("dp") * lax.axis_size("seq") + lax.axis_index("seq")
     piece, width = g_query.shape
@@ -886,8 +917,10 @@
         return pltpu.roll(row, width - at * length, 1)[0, :length]
 
     b_query, b_value, b_out, b_outer, gain_one, shift_one, gain_two, shift_two, b_inner = vectors
-    for at, out in enumerate((b_query, b_value, gain_one, shift_one)):
+    for at, out in enumerate((b_query, b_value)):
         out[...] = entries(sums_ref[heads + at : heads + at + 1], device, piece)
+    for at, out in enumerate((gain_one, shift_one)):
+        out[...] = entries(scale_ref[at : at + 1], device, piece)
     for at, out in enumerate((b_out, b_outer, gain_two, shift_two)):
         row = 3 * piece + at
         out[...] = entries(early_ref[row : row + 1], device, piece)
@@ -896,11 +929,9 @@
     labels = table.shape[0]
     turned = pltpu.roll(sums_ref[:, :WINDOW], WINDOW - HALO + R, 1).T
     table[...] = turned[:labels, :heads]
-    for copy in copies:
-        copy.wait()
-
-
-def small_results(heads, early, late, outer, inner, sums, *big):
+
+
+def small_results(heads, early, late, outer, inner, sums, scales):
     width = early.shape[1]
     piece = width // 32
     shape = jax.ShapeDtypeStruct
@@ -909,15 +940,13 @@
     outs += [shape((piece, 4 * width), F32), shape((4 * piece, width), F32)]
     outs += [shape((piece,), F32)] * 8 + [shape((4 * piece,), F32)]
     outs += [shape((2 * R + 1, heads), F32)]
-    there = [pl.BlockSpec(memory_space=pl.ANY)] * len(big)
     return pl.pallas_call(
         functools.partial(small_kernel, heads),
-        in_specs=[whole] * 5 + there,
-        out_specs=[whole] * len(outs) + there,
-        out_shape=outs + [shape(part.shape, part.dtype) for part in big],
-        scratch_shapes=[pltpu.SemaphoreType.DMA((len(big),))],
+        in_specs=[whole] * 6,
+        out_specs=[whole] * len(outs),
+        out_shape=outs,
         name="small_results",
-    )(early, late, outer, inner, sums, *big)
+    )(early, late, outer, inner, sums, scales)
 
 
 def has_plan():
@@ -1180,29 +1209,29 @@
 OUTER, INNER = 0, 1
 FFN_PLAN = (
     ((1, 0), OUTER, "add_core", 0),
+    ((2, 0), OUTER, "add_core", 1),
     ((2, 0), OUTER, "add_first", 0),
-    ((2, 0), OUTER, "add_core", 1),
-    ((2, 1), OUTER, "add_second", 0),
     ((2, 1), INNER, "add_core", 0),
     ((2, 1), INNER, "add_core", 1),
     ((2, 1), INNER, "add_core", 2),
     ((2, 1), INNER, "add_core", 3),
     ((3, 0), OUTER, "add_first", 1),
+    ((3, 0), OUTER, "add_second", 0),
     ((3, 0), OUTER, "add_core", 2),
-    ((3, 1), OUTER, "add_second", 1),
-    ((3, 1), INNER, "add_first", 0),
-    ((3, 1), INNER, "add_first", 1),
     ((4, 0), OUTER, "add_core", 3),
+    ((4, 0), INNER, "add_first", 0),
+    ((4, 0), INNER, "add_first", 1),
     ((4, 0), OUTER, "add_first", 2),
-    ((4, 0), INNER, "add_second", 0),
-    ((4, 0), INNER, "add_first", 2),
-    ((4, 0), INNER, "add_second", 1),
-    ((4, 0), INNER, "add_first", 3),
-    ((4, 1), OUTER, "add_second", 2),
-    ((4, 1), OUTER, "add_first", 3),
-    ((4, 1), INNER, "add_second", 2),
+    ((4, 0), OUTER, "add_second", 1),
+    ((4, 1), INNER, "add_first", 2),
+    ((4, 1), INNER, "add_first", 3),
+    ((4, 1), INNER, "add_second", 0),
+    ((4, 1), INNER, "add_second", 1),
+    ((4, 2), OUTER, "add_first", 3),
+    ((4, 2), OUTER, "add_second", 2),
+    ((4, 2), INNER, "add_second", 2),
+    ((4, 2), INNER, "add_second", 3),
     ((4, 2), OUTER, "add_second", 3),
-    ((4, 2), INNER, "add_second", 3),
 )
 
 
@@ -1775,11 +1804,7 @@
             g_s2,
             g_b_inner,
             table_total,
-            long_grad,
-            long_result,
-        ) = small_results(
-            heads, late[2], late[0], early[1], early[2], late[1], long_grad, long_result
-        )
+        ) = small_results(heads, late[3], late[0], early[1], early[2], late[1], late[2])
     else:
         devices = data_count * seq_count
         own_part = lambda vector: lax.dynamic_slice_in_dim(
@@ -1794,8 +1819,9 @@
             )
             for g in (g_outer, g_inner, g_out, *late[:3])
         )
-        vectors, sums = lax.psum((vectors, late[3]), ("dp", "seq"))
-        g_b_query, g_b_value, g_g1, g_s1 = (own_part(sums[heads + i]) for i in range(4))
+        vectors, sums, scales = lax.psum((vectors, *late[3:]), ("dp", "seq"))
+        g_b_query, g_b_value = (own_part(sums[heads + i]) for i in range(2))
+        g_g1, g_s1 = (own_part(scales[i]) for i in range(2))
         g_b_out, g_b_outer, g_g2, g_s2 = (own_part(vectors[i]) for i in range(4))
         g_b_inner = own_part(vectors[4:].reshape(-1))
         table_total = sums[:heads, HALO - R : HALO - R + labels].T

time: 261 us -> 184 us (0.70)
  Pallas kernels: 254 us -> 174 us
  local copies, waits for them, and re-layouts: 5.41 us -> 8.68 us
    pallas_call x1, Pallas kernels: 74.9 us -> 2.42 us  [small_results(): pl.pallas_call(functools.partial(small_kernel, heads), in_specs=[whole] *...]
    pallas_call x1, Pallas kernels: 61 us -> 57.1 us  [feed_forward(): pl.pallas_call(functools.partial(ffn_kernel, sizes, planned), grid=(4,),...]
    unnamed x8 -> x12, local copies, waits for them, and re-layouts: 5.41 us -> 8.68 us
    pallas_call x1, Pallas kernels: 45 us -> 42 us  [last_part(): pl.pallas_call(functools.partial(late_kernel, sizes, planned), in_specs=[...]
where the time goes in v2:
time: 184 us
  Pallas kernels  174 us (95%)
  local copies, waits for them, and re-layouts  8.68 us (5%)
    pallas_call x1, Pallas kernels, feed_forward(): pl.pallas_call(functools.partial(ffn_kernel, sizes, planned), grid=(4,),...  57.1 us
    pallas_call x1, Pallas kernels, attend_back(): pl.pallas_call(functools.partial(back_kernel, sizes, early_rows), grid=(2...  43 us
    pallas_call x1, Pallas kernels, last_part(): pl.pallas_call(functools.partial(late_kernel, sizes, planned), in_specs=[...  42 us
    pallas_call x1, Pallas kernels, attend(): pl.pallas_call(functools.partial(attend_kernel, sizes), in_specs=[pl.Bloc...  29.4 us
    unnamed x12, local copies, waits for them, and re-layouts  8.68 us

profile of v2, /device:TPU:0, one launch (start us, length us, event | category | flops | bytes accessed | tf_op | source)
XLA Modules:
  0.0 184.0 jit_solution(7004727295148752182)
XLA Ops:
  1.3 1.5 copy.41.rel_ref
  2.8 29.4 %attend.1 = (bf16[768,768]{1,0:T(8,128)(2,1)}, bf16[768,768]{1,0:T(8,128)(2,1)}, bf16[768,768]{1,0:T(8,128)(2,1)}, bf16[256,768]{1,0:T(8,128)(2,1)}, bf16[256,76...) custom-call(s32[1]{0:T(128)S(6)} %copy.47.len_ref, ...), custom_call_target="tpu_custom_call" | custom-call | tf_op jit(solution)/shard_map/attend/pallas_call | solution.py:345
  32.2 57.1 %feed_forward.1 = (bf16[512,768]{1,0:T(8,128)(2,1)}, bf16[64,768]{1,0:T(8,128)(2,1)}, f32[576,768]{1,0:T(8,128)}, bf16[576,768]{1,0:T(8,128)(2,1)}, bf16[256,768...) custom-call(s32[1]{0:T(128)S(6)} %copy.47.len_ref, ...), custom_call_target="tpu_custom_call" | custom-call | tf_op jit(solution)/shard_map/feed_forward/pallas_call | solution.py:1306
  89.3 43.0 %attend_back.1 = (bf16[576,768]{1,0:T(8,128)(2,1)}, bf16[576,768]{1,0:T(8,128)(2,1)}, bf16[576,768]{1,0:T(8,128)(2,1)}, f32[6,2,512]{2,1,0:T(2,128)}, bf16[230,7...) custom-call(s32[1]{0:T(128)S(6)} %copy.47.len_ref, ...), custom_call_target="tpu_custom_call" | custom-call | tf_op jit(solution)/shard_map/attend_back/pallas_call | solution.py:1673
  132.3 42.0 %last_part.1 = (f32[512,768]{1,0:T(8,128)}, f32[230,768]{1,0:T(8,128)}, f32[80,768]{1,0:T(8,128)}, f32[16,768]{1,0:T(8,128)}, f32[8,768]{1,0:T(8,128)}, /*index=5*/f32[80,768]{1,0:T(8,128)}) custom-call(bf16[512,768]{1,0:T(8,128)(2,1)} %bitcast.10, bf16[256,768]{1,0:T(8,128)(2,1)} %get-tuple-element.70.glob_ref, bf16[576,768]{1,0:T(8,128)(2,1)} %get-tuple-element.88.dq_ref, ...), custom_call_target="tpu_custom_call" | custom-call | tf_op jit(solution)/shard_map/last_part/pallas_call | solution.py:887
  174.3 0.0 copy-start.1
  174.3 2.8 %copy.42 = f32[1,230,768]{2,0,1:T(1,128)} copy(f32[1,230,768]{2,1,0:T(8,128)} %bitcast.14) | data formatting | bytes 1413120
  177.1 0.0 copy-start.2
  177.1 2.4 %small_results.1 = (f32[24,768]{1,0:T(8,128)}, f32[24,768]{1,0:T(8,128)}, f32[24,768]{1,0:T(8,128)}, f32[24,768]{1,0:T(8,128)}, f32[24,3072]{1,0:T(8,128)}, /*in...) custom-call(f32[80,768]{1,0:T(8,128)} %get-tuple-element.96.early_re, ...), custom_call_target="tpu_custom_call" | custom-call | tf_op jit(solution)/shard_map/small_results/pallas_call | solution.py:943
  179.5 0.0 copy-start
  179.5 1.7 copy.43
  181.2 0.0 copy-done.1
  181.2 0.9 copy.48
  182.1 0.0 copy-done.2
  182.1 0.7 copy.49
  182.9 0.0 copy-done
  182.9 1.1 copy.50
Async XLA Ops:
  174.3 6.9 %copy-start.1 = (bf16[512,768]{1,0:T(8,128)(2,1)S(1)}, bf16[512,768]{1,0:T(8,128)(2,1)}, u32[]{:S(2)}) copy-start(bf16[512,768]{1,0:T(8,128)(2,1)} %get-tuple-element.72) | copy-start | bytes 2359300
  177.1 5.0 %copy-start.2 = (bf16[230,768]{1,0:T(8,128)(2,1)S(1)}, bf16[230,768]{1,0:T(8,128)(2,1)}, u32[]{:S(2)}) copy-start(bf16[230,768]{1,0:T(8,128)(2,1)} %get-tuple-element.87) | copy-start | bytes 1059844
  179.5 3.3 %copy-start = (f32[512,768]{1,0:T(8,128)S(1)}, f32[512,768]{1,0:T(8,128)}, u32[]{:S(2)}) copy-start(f32[512,768]{1,0:T(8,128)} %get-tuple-element.94) | copy-start | bytes 4718596
